TPU v7x, 128 devices: a whole 4x4x4 slice. The times are simulated.
128 devices in a mesh: dp: 8 (over x_hi, y), fsdp: 16 (over x_lo, z, core).
Axes of the slice: x: 4 (x_hi: 2, x_lo: 2; x = x_hi * 2 + x_lo), y: 4, z: 4, core: 2. Of those that a mesh axis runs over, the one named last changes fastest.
Arguments:
- queries: bfloat16 [16384, 2048], P(('dp', 'fsdp')), may hold values from -16 to 16
- doc_kv: bfloat16 [2, 8, 512, 2048], P(None, 'dp', 'fsdp'), may hold values from -12 to 12
- residual: bfloat16 [16384, 4096], P(('dp', 'fsdp')), may hold values from -25 to 25
- out_weight: bfloat16 [2048, 4096], P(None, 'fsdp'), may hold values from -0.125 to 0.125
- out_gain: float32 [4096], replicated, may hold values from 0.1 to 1.9
- head: bfloat16 [16384, 4096], P('fsdp')
- source: int32 [8], replicated, may hold values from 0 to 7, each once
- lengths: int32 [8, 8], P('dp'), may hold values from 1 to 256, 1280 in all within a row
- sampled: int32 [16384], P(('dp', 'fsdp')), may hold values from 0 to 16383
- old_logprob: float32 [16384], P(('dp', 'fsdp')), may hold values from -13 to -7
Outputs:
- log_ratio: float32 [16384], P(('dp', 'fsdp'))
- kl_term: float32 [16384], P(('dp', 'fsdp'))
Inputs may be any that keep to these rules, and one draw needn't show every extreme that they name: Each row of lengths sums to 1280. `source`: each document appears once.
All inputs are finite; a program needn't handle non-finite values.
Results may differ from a plain program's by a relative error of at most 0.0028.
Values may be sent and summed in bfloat16 or wider, within the bound.
A program may use at most 128 MiB of HBM per device.

v0:
```python
import jax
import jax.numpy as jnp
from jax import lax
from jax.sharding import PartitionSpec as P

HEADS = 8


def joined(value, axis, join):
    pieces = jax.tree.map(lambda part: lax.all_gather(part, axis), value)
    head = jax.tree.map(lambda part: part[0], pieces)
    tail = jax.tree.map(lambda part: part[1:], pieces)
    total, _ = lax.scan(lambda total, share: (join(total, share), None), head, tail)
    return total


def attend(query_rows, keys, values, heads):
    count = query_rows.shape[0]
    width = query_rows.shape[1]
    depth = width // heads
    q3 = query_rows.reshape(count, heads, depth)
    k3 = keys.reshape(keys.shape[0], heads, depth)
    v3 = values.reshape(values.shape[0], heads, depth)
    scores = jnp.einsum("thd,lhd->htl", q3, k3, preferred_element_type=jnp.float32) * float(
        depth
    ) ** (-0.5)
    largest = jnp.max(scores, axis=2, keepdims=True)
    raised = jnp.exp(scores - largest)
    weights = (raised / jnp.sum(raised, axis=2, keepdims=True)).astype(jnp.bfloat16)
    mixed = jnp.einsum("htl,lhd->thd", weights, v3, preferred_element_type=jnp.float32)
    return mixed.reshape(count, width).astype(jnp.bfloat16)


def combine_totals(first, second):
    highest = jnp.maximum(first[0], second[0])
    total = first[1] * jnp.exp(first[0] - highest) + second[1] * jnp.exp(second[0] - highest)
    return (highest, total, first[2] + second[2])


def on_device(
    queries, doc_kv, residual, out_weight, out_gain, head, source, lengths, sampled, old_logprob
):
    shard_pos = lax.axis_index("fsdp")
    row_pos = lax.axis_index("dp")
    tok_rows = queries.shape[0]
    every_doc = lax.all_gather(doc_kv, "dp", axis=1, tiled=True)
    chosen = lax.dynamic_index_in_dim(every_doc, source[row_pos], 1, keepdims=False)
    whole_doc = lax.all_gather(chosen, "fsdp", axis=1, tiled=True)
    attended = attend(queries, whole_doc[0], whole_doc[1], HEADS)
    mixed = jnp.dot(
        attended,
        lax.all_gather(out_weight, "fsdp", axis=1, tiled=True),
        preferred_element_type=jnp.float32,
    )
    summed = mixed + residual.astype(jnp.float32)
    scale = lax.rsqrt(jnp.mean(summed * summed, axis=1, keepdims=True) + 1e-06)
    hidden = (summed * scale * out_gain[None, :]).astype(jnp.bfloat16)
    group_hidden, group_ids = (
        lax.all_gather(hidden, "fsdp", axis=0, tiled=True),
        lax.all_gather(sampled, "fsdp", axis=0, tiled=True),
    )
    vocab_rows = head.shape[0]
    logits = lax.dot_general(
        group_hidden, head, (((1,), (1,)), ((), ())), preferred_element_type=jnp.float32
    )
    columns = jnp.arange(vocab_rows, dtype=jnp.int32) + shard_pos * vocab_rows
    matches = columns[None, :] == group_ids[:, None]
    picked = jnp.sum(jnp.where(matches, logits, 0.0), axis=1)
    largest = jnp.max(logits, axis=1)
    own_start = shard_pos * tok_rows
    total = jnp.sum(jnp.exp(logits - largest[:, None]), axis=1)
    highest, total, picked = joined((largest, total, picked), "fsdp", combine_totals)
    highest = lax.dynamic_slice_in_dim(highest, own_start, tok_rows, 0)
    total = lax.dynamic_slice_in_dim(total, own_start, tok_rows, 0)
    picked = lax.dynamic_slice_in_dim(picked, own_start, tok_rows, 0)
    new_logprob = picked - (highest + jnp.log(total))
    position = shard_pos % 2 * tok_rows + jnp.arange(tok_rows, dtype=jnp.int32)
    limit = lax.dynamic_index_in_dim(lengths[0], shard_pos // 2, 0, keepdims=False)
    live = position < limit
    log_ratio = jnp.where(live, new_logprob - old_logprob, jnp.float32(0.0))
    gap = jnp.clip(old_logprob - new_logprob, -3.0, 3.0)
    kl_term = jnp.where(live, jnp.exp(gap) - gap - 1.0, jnp.float32(0.0))
    return (log_ratio, kl_term)


def solution(mesh):
    return jax.shard_map(
        on_device,
        mesh=mesh,
        in_specs=(
            P(("dp", "fsdp"), None),
            P(None, "dp", "fsdp", None),
            P(("dp", "fsdp"), None),
            P(None, "fsdp"),
            P(),
            P("fsdp", None),
            P(),
            P("dp", None),
            P(("dp", "fsdp")),
            P(("dp", "fsdp")),
        ),
        out_specs=(P(("dp", "fsdp")), P(("dp", "fsdp"))),
        check_vma=False,
    )
```

profile of v0, /device:TPU:1, one launch (start us, length us, event | category | flops | bytes accessed | tf_op | source)
XLA Modules:
  0.0 398.0 jit_solution(15612936221681823901)
XLA Ops:
  7.2 0.0 copy-start
  7.2 0.0 all-gather.10.cloned.1.call-start
  7.2 1.9 copy.19
  9.2 0.0 all-gather.10.cloned.1.call-update
  9.2 0.0 all-gather.16.cloned.1.call-start
  9.2 1.2 dynamic_slice.31
  12.4 54.9 %all-gather.10.cloned.1.call-done = bf16[2,8,32,2048]{3,0,1,2:T(2,128)(2,1)} async-done(((bf16[2,1,32,2048]{3,0,1,2:T(2,128)(2,1)}), bf16[2,8,32,2048]{3,0,1,2:T(2,128)(2,1)}) %all-gather.10.cloned.1.call-update) | async-done | bytes 2097168 | tf_op jit(solution)/shard_map/all_gather | solution.py:46
  67.3 1.8 constant_dynamic-slice_fusion.3
  69.2 0.0 all-gather.16.cloned.1.call-update
  69.2 0.0 all-gather.12.cloned.1.call-start
  69.3 0.7 all-gather.12.cloned.1.call-update
  69.9 0.0 all-gather.14.cloned.1.call-start
  70.0 35.5 %all-gather.16.cloned.1.call-done = bf16[2,1,512,2048]{3,0,1,2:T(2,128)(2,1)} async-done(((bf16[2,1,32,2048]{3,0,1,2:T(2,128)(2,1)}), bf16[2,1,512,2048]{3,0,1,2:T(2,128)(2,1)}) %all-gather.16.cloned.1.call-update) | async-done | bytes 4194320 | tf_op jit(solution)/shard_map/all_gather | solution.py:48
  105.5 10.3 %fusion.19 = (bf16[1,1,512,2048]{3,0,1,2:T(2,128)(2,1)}, bf16[1,1,512,2048]{3,0,1,2:T(2,128)(2,1)}) fusion(bf16[2,1,512,2048]{3,0,1,2:T(2,128)(2,1)} %all-gather.16.cloned.1.call-done), kind=kLoop, calls=%fused_computation.34 | loop fusion | bytes 8388608 | tf_op jit(solution)/shard_map/slice | solution.py:49
  115.8 9.1 %copy.27 = bf16[1,1,512,2048]{2,3,1,0:T(8,128)(2,1)S(1)} copy(bf16[1,1,512,2048]{3,0,1,2:T(2,128)(2,1)} %get-tuple-element.66) | data formatting | bytes 4194304
  125.0 0.0 copy-start.5
  125.0 10.7 %copy.20 = bf16[1,1,512,2048]{2,3,1,0:T(8,128)(2,1)} copy(bf16[1,1,512,2048]{3,0,1,2:T(2,128)(2,1)} %get-tuple-element.67) | data formatting | bytes 4194304 | tf_op jit(solution)/shard_map/slice | solution.py:49
  135.7 0.0 copy-done.5
  135.7 0.8 fusion.7
  136.6 0.0 copy-start.3
  136.6 1.3 copy-done.3
  137.9 0.0 copy-start.2
  137.9 0.6 fusion.20
  138.4 1.0 copy-done.2
  139.5 0.0 copy-start.4
  139.5 4.3 %convolution_convert_fusion = bf16[8,256,128]{2,1,0:T(8,128)(2,1)} fusion(bf16[512,8,256]{0,2,1:T(8,128)(2,1)S(1)} %bitcast.48, f32[8,128]{1,0:T(8,128)S(1)} %fusion.20, f32[8,512,128]{2,1,0:T(8,128)} %copy-done.3), kind=kOutput, calls=%fused_computation.16 | convolution fusion | flops 271320576 | bytes 4722688 | tf_op jit(solution)/shard_map/htl,lhd->thd/dot_general | solution.py:30
  143.7 63.0 %all-gather.12.cloned.1.call-done = bf16[2048,4096]{1,0:T(8,128)(2,1)} async-done(((bf16[2048,256]{1,0:T(8,128)(2,1)}), bf16[2048,4096]{1,0:T(8,128)(2,1)}) %all-gather.12.cloned.1.call-update) | async-done | bytes 16777232 | tf_op jit(solution)/shard_map/all_gather | solution.py:52
  206.7 0.0 copy-done.4
  206.7 0.0 copy-start.6
  206.7 8.6 %multiply_reduce_fusion = (f32[128]{0:T(128)S(1)}, f32[128,4096]{1,0:T(8,128)S(1)}) fusion(bf16[128,4096]{1,0:T(8,128)(2,1)S(1)} %copy-done.4, bf16[128,2048]{0,1:T(8,128)(2,1)} %bitcast.52, bf16[2048,4096]{1,0:T(8,128)(2,1)} %all-gather.12.cloned.1.call-done), kind=kOutput, calls=%fused_computation.13 | convolution fusion | flops 2149580800 | bytes 20447744 | tf_op jit(solution)/shard_map/dot_general | solution.py:50
  215.3 0.0 copy-done.6
  215.3 0.0 copy-start.8
  215.3 1.3 multiply_convert_fusion
  216.6 0.0 all-gather.14.cloned.1.call-update
  216.6 0.0 copy-done
  216.6 0.6 constant_dynamic-slice_fusion.4
  217.3 0.0 copy-done.8
  217.3 17.7 %all-gather.4 = s32[16,1,128]{2,1,0:T(1,128)S(1)} all-gather(s32[1,1,128]{2,1,0:T(1,128)S(1)} %bitcast.55), channel_id=1, replica_groups=mesh['dp'=8,'fsdp'=16] {'fsdp'}, dimensions={0}, use_global_device_ids=true | all-gather | bytes 8704 | tf_op jit(solution)/shard_map/all_gather | solution.py:60
  235.0 73.2 %all-gather.14.cloned.1.call-done = bf16[2048,4096]{1,0:T(8,128)(2,1)} async-done(((bf16[128,4096]{1,0:T(8,128)(2,1)}), bf16[2048,4096]{1,0:T(8,128)(2,1)}) %all-gather.14.cloned.1.call-update) | async-done | bytes 16777232 | tf_op jit(solution)/shard_map/all_gather | solution.py:59
  308.2 22.8 %fusion.21 = (f32[2048]{0:T(1024)S(1)}, f32[2048,1024]{0,1:T(8,128)S(1)}) fusion(bf16[2048,4096]{1,0:T(8,128)(2,1)} %all-gather.14.cloned.1.call-done, bf16[1024,4096]{1,0:T(8,128)(2,1)} %param.17), kind=kOutput, calls=%fused_computation.36 | convolution fusion | flops 17181964288 | bytes 33562624 | tf_op jit(solution)/shard_map/dot_general | solution.py:63
  331.0 19.4 %all-gather.1 = f32[32768]{0:T(1024)S(1)} all-gather(f32[2048]{0:T(1024)S(1)} %get-tuple-element.70), channel_id=3, replica_groups=mesh['dp'=8,'fsdp'=16] {'fsdp'}, dimensions={0}, use_global_device_ids=true | all-gather | bytes 139264 | tf_op jit(solution)/shard_map/all_gather | solution.py:10
  350.5 0.0 copy-start.1
  350.5 2.5 select_reduce_fusion
  352.9 0.0 copy-start.7
  352.9 16.6 %all-gather.2 = f32[32768]{0:T(1024)S(1)} all-gather(f32[2048]{0:T(1024)S(1)} %get-tuple-element.45), channel_id=4, replica_groups=mesh['dp'=8,'fsdp'=16] {'fsdp'}, dimensions={0}, use_global_device_ids=true | all-gather | bytes 139264 | tf_op jit(solution)/shard_map/all_gather | solution.py:10
  369.6 17.9 %all-gather.3 = f32[32768]{0:T(1024)S(1)} all-gather(f32[2048]{0:T(1024)S(1)} %get-tuple-element.44), channel_id=5, replica_groups=mesh['dp'=8,'fsdp'=16] {'fsdp'}, dimensions={0}, use_global_device_ids=true | all-gather | bytes 139264 | tf_op jit(solution)/shard_map/all_gather | solution.py:10
  387.6 1.5 while.14
  389.1 0.0 copy-done.7
  389.1 1.2 compare_select_fusion
  390.4 1.1 compare_select_fusion.1
  391.5 0.0 copy-done.1
  (71 shorter events, 0.9 us)
Async XLA Ops:
  7.2 209.5 %copy-start = (s32[1,8]{1,0:T(1,128)S(1)}, s32[1,8]{1,0:T(1,128)}, u32[]{:S(2)}) copy-start(s32[1,8]{1,0:T(1,128)} %param.19) | copy-start | bytes 100
  7.2 60.2 %all-gather.10.cloned.1.call-start = ((), (), s32[]{:S(2)}) async-start(), calls=%async_computation | async-start | bytes 2359296 | tf_op jit(solution)/shard_map/all_gather | solution.py:46
  9.2 96.4 %all-gather.16.cloned.1.call-start = ((), (), s32[]{:S(2)}) async-start(), calls=%async_computation.3 | async-start | bytes 4456448 | tf_op jit(solution)/shard_map/all_gather | solution.py:48
  69.2 137.5 %all-gather.12.cloned.1.call-start = ((), (), s32[]{:S(2)}) async-start(), calls=%async_computation.1 | async-start | bytes 17825792 | tf_op jit(solution)/shard_map/all_gather | solution.py:52
  69.9 238.3 %all-gather.14.cloned.1.call-start = ((), (), s32[]{:S(2)}) async-start(), calls=%async_computation.2 | async-start | bytes 17825792 | tf_op jit(solution)/shard_map/all_gather | solution.py:59
  125.0 10.7 %copy-start.5 = (bf16[128,2048]{1,0:T(8,128)(2,1)S(1)}, bf16[128,2048]{1,0:T(8,128)(2,1)}, u32[]{:S(2)}) copy-start(bf16[128,2048]{1,0:T(8,128)(2,1)} %param.12) | copy-start | bytes 1572868
  136.6 1.3 copy-start.3
  137.9 1.6 copy-start.2
  139.5 67.2 %copy-start.4 = (bf16[128,4096]{1,0:T(8,128)(2,1)S(1)}, bf16[128,4096]{1,0:T(8,128)(2,1)}, u32[]{:S(2)}) copy-start(bf16[128,4096]{1,0:T(8,128)(2,1)} %param.14) | copy-start | bytes 3145732
  206.7 8.6 %copy-start.6 = (f32[4096]{0:T(1024)S(1)}, f32[4096]{0:T(1024)}, u32[]{:S(2)}) copy-start(f32[4096]{0:T(1024)} %param.16) | copy-start | bytes 49156
  215.3 2.0 copy-start.8
  350.5 41.1 %copy-start.1 = (s32[1,8]{1,0:T(1,128)S(1)}, s32[1,8]{1,0:T(1,128)}, u32[]{:S(2)}) copy-start(s32[1,8]{1,0:T(1,128)} %param.19) | copy-start | bytes 100
  352.9 36.2 %copy-start.7 = (f32[128]{0:T(128)S(1)}, f32[128]{0:T(128)}, u32[]{:S(2)}) copy-start(f32[128]{0:T(128)} %param.21) | copy-start | bytes 1540
Sparse Core Ops, SparseCore 0:
  10.2 57.1 all-gather.9
  69.3 36.1 all-gather.15
  107.2 99.4 all-gather.11
  216.7 91.4 all-gather.13
where the time goes:
time: 399 us; the launch traced here: 398 us
  waiting for transfers between devices  227 us (57%)
  blocking collectives  71.7 us (18%)
  local copies, waits for them, and re-layouts  38.8 us (10%)
  matrix products  36.5 us (9%)
  between operations  15.9 us (4%)
  other arithmetic  6.93 us (2%)
    all_gather x1, waiting for transfers between devices, on_device(): lax.all_gather(hidden, 'fsdp', axis=0, tiled=True)  73.2 us
    all_gather x1, waiting for transfers between devices, on_device(): lax.all_gather(out_weight, 'fsdp', axis=1, tiled=True)  63 us
    all_gather x1, waiting for transfers between devices, on_device(): every_doc = lax.all_gather(doc_kv, 'dp', axis=1, tiled=True)  54.9 us
    all_gather x3, blocking collectives, joined(): pieces = jax.tree.map(lambda part: lax.all_gather(part, axis), value)  54 us
    all_gather x1, waiting for transfers between devices, on_device(): whole_doc = lax.all_gather(chosen, 'fsdp', axis=1, tiled=True)  35.5 us
    dot_general x1, matrix products, on_device(): lax.dot_general(group_hidden, head, (((1,), (1,)), ((), ())), preferred_e...  22.8 us
    slice x2, local copies, waits for them, and re-layouts, on_device(): attended = attend(queries, whole_doc[0], whole_doc[1], HEADS)  21 us
    all_gather x1, blocking collectives, on_device(): lax.all_gather(sampled, 'fsdp', axis=0, tiled=True)  17.7 us
  transfers between devices with their start and end apart: 4, of which 4 were waited for; matrix products, arithmetic and copies ran while one was open for 9% of the time, Pallas kernels for 0%

commit v1 on v0

v1 whole, which is shorter than its diff:
```python
import jax
import jax.numpy as jnp
from jax import lax
from jax.experimental import pallas as pl
from jax.experimental.pallas import tpu as pltpu
from jax.sharding import PartitionSpec as P

HEADS = 8
DEPTH = 256
GROUP = 16
ROWS = 8
MESH = pl.DeviceIdType.MESH
PIECES = 4


class Gather:
    def __init__(self, me, buf, own, send_sem, recv_sem, pieces):
        self.me, self.buf, self.own = me, buf, own
        self.send_sem, self.recv_sem = send_sem, recv_sem
        self.pieces = pieces
        self.rows = buf.shape[2] // pieces
        x, z, core = me // 8, (me // 2) % 4, me % 2

        def slot(dx, dz):
            return ((x + dx) % 2) * 8 + ((z + dz) % 4) * 2 + core

        self.x, self.zp, self.zm, self.z2 = slot(1, 0), slot(0, 1), slot(0, 3), slot(0, 2)
        self.xzp, self.xzm, self.xz2 = slot(1, 1), slot(1, 3), slot(1, 2)
        self.core = me + 1 - 2 * core

    def at(self, ref, slot, half, p):
        return ref.at[slot, half, pl.ds(p * self.rows, self.rows)]

    def send(self, slot, half, p, *targets, own=False):
        dst = self.at(self.buf, slot, half, p)
        src = self.own.at[half, pl.ds(p * self.rows, self.rows)] if own else dst
        for target in targets:
            pltpu.make_async_remote_copy(
                src_ref=src,
                dst_ref=dst,
                send_sem=self.send_sem,
                recv_sem=self.recv_sem.at[slot, half, p],
                device_id={"fsdp": target},
                device_id_type=MESH,
            ).start()

    def wait(self, slot, half, p):
        view = self.at(self.buf, slot, half, p)
        pltpu.make_async_copy(view, view, self.recv_sem.at[slot, half, p]).wait()

    def each(self, step):
        if self.pieces == 1:
            step(0)
        else:
            pl.loop(0, self.pieces)(step)

    def wave1(self):
        def first(p):
            self.send(self.me, 0, p, self.x, own=True)
            self.send(self.me, 1, p, self.zp, self.zm, own=True)

        def second(p):
            self.send(self.me, 1, p, self.x, self.core, own=True)
            self.send(self.me, 0, p, self.zp, self.zm, self.core, own=True)

        self.each(first)
        self.each(second)

    def wave2(self):
        def step(p):
            self.wait(self.x, 0, p)
            self.send(self.x, 0, p, self.zp, self.zm, self.core)
            self.wait(self.zp, 1, p)
            self.send(self.zp, 1, p, self.zm, self.x, self.core)
            self.wait(self.zm, 1, p)
            self.send(self.zm, 1, p, self.x, self.core)

        self.each(step)

    def wave3(self):
        def step(p):
            self.wait(self.zm, 0, p)
            self.send(self.zm, 0, p, self.zp, self.core)
            self.wait(self.zp, 0, p)
            self.send(self.zp, 0, p, self.core)
            self.wait(self.x, 1, p)
            self.send(self.x, 1, p, self.core)

        def later(p):
            self.wait(self.z2, 1, p)
            self.send(self.z2, 1, p, self.x, self.core)
            self.wait(self.xzm, 0, p)
            self.send(self.xzm, 0, p, self.zp, self.core)
            self.wait(self.xzp, 0, p)
            self.send(self.xzp, 0, p, self.core)

        self.each(step)
        self.each(later)

    def wave4(self):
        def step(p):
            for slot, half in ((self.xzp, 1), (self.xzm, 1), (self.z2, 0)):
                self.wait(slot, half, p)
                self.send(slot, half, p, self.core)

        def later(p):
            for slot, half in ((self.xz2, 0), (self.xz2, 1)):
                self.wait(slot, half, p)
                self.send(slot, half, p, self.core)

        self.each(step)
        self.each(later)

    def wait_slot(self, slot):
        for half in range(2):
            self.each(lambda p: self.wait(slot, half, p))

    def wait_siblings(self):
        other = self.core % 2

        @pl.loop(0, GROUP // 2)
        def _(k):
            self.wait_slot(2 * k + other)

    def drain(self):
        view = self.buf.at[pl.ds(0, 15)]
        pltpu.make_async_copy(view, view, self.send_sem).wait()


def kernel(
    source,
    lengths,
    ids,
    old,
    gain,
    q_hbm,
    doc_hbm,
    res_hbm,
    w_hbm,
    head_hbm,
    ratio_out,
    kl_out,
    head,
    wbuf,
    hbuf,
    dbuf,
    kv,
    q,
    res,
    att,
    summed,
    logits,
    idbuf,
    stat_out,
    stat_in,
    local_sems,
    w_send,
    w_recv,
    h_send,
    h_recv,
    kv_send,
    kv_recv,
    dp_send,
    dp_recv,
    id_send,
    id_recv,
    stat_send,
    stat_recv,
):
    row = lax.axis_index("dp")
    me = lax.axis_index("fsdp")

    barrier = pltpu.get_barrier_semaphore()

    @pl.loop(1, GROUP)
    def _(j):
        pl.semaphore_signal(barrier, inc=1, device_id={"fsdp": (me + j) % GROUP}, device_id_type=MESH)

    @pl.loop(1, ROWS)
    def _(j):
        pl.semaphore_signal(barrier, inc=1, device_id={"dp": (row + j) % ROWS}, device_id_type=MESH)

    locals_ = [
        pltpu.make_async_copy(doc_hbm, dbuf.at[row], local_sems.at[0]),
        pltpu.make_async_copy(q_hbm, q, local_sems.at[1]),
        pltpu.make_async_copy(res_hbm, res, local_sems.at[2]),
        pltpu.make_async_copy(w_hbm, wbuf.at[me], local_sems.at[3]),
        pltpu.make_async_copy(head_hbm, head, local_sems.at[4]),
    ]
    for copy in locals_:
        copy.start()
    idbuf[me] = jnp.broadcast_to(ids[...], (8, 128))

    pl.semaphore_wait(barrier, GROUP + ROWS - 2)

    @pl.loop(1, ROWS)
    def _(j):
        pltpu.make_async_remote_copy(
            src_ref=doc_hbm,
            dst_ref=dbuf.at[row],
            send_sem=dp_send,
            recv_sem=dp_recv.at[row],
            device_id={"dp": (row + j) % ROWS},
            device_id_type=MESH,
        ).start()

    wg = Gather(me, wbuf, w_hbm, w_send, w_recv, PIECES)
    hg = Gather(me, hbuf, hbuf.at[me], h_send, h_recv, PIECES)
    dg = Gather(me, kv, kv.at[me], kv_send, kv_recv, 1)
    wg.wave1()

    @pl.loop(1, GROUP)
    def _(j):
        pltpu.make_async_remote_copy(
            src_ref=idbuf.at[me],
            dst_ref=idbuf.at[me],
            send_sem=id_send,
            recv_sem=id_recv.at[me],
            device_id={"fsdp": (me + j) % GROUP},
            device_id_type=MESH,
        ).start()

    wg.wave2()

    @pl.loop(1, ROWS)
    def _(j):
        other = (row + j) % ROWS
        pltpu.make_async_copy(dbuf.at[other], dbuf.at[other], dp_recv.at[other]).wait()

    locals_[0].wait()
    kv[me] = dbuf[source[row]]
    dg.wave1()
    wg.wave3()
    dg.wave2()
    dg.wave3()
    wg.wave4()
    dg.wave4()
    dg.wait_siblings()

    locals_[1].wait()

    @pl.loop(0, HEADS)
    def _(h):
        columns = pl.ds(pl.multiple_of(h * DEPTH, DEPTH), DEPTH)
        keys = kv[:, 0, :, columns].reshape(-1, DEPTH)
        values = kv[:, 1, :, columns].reshape(-1, DEPTH)
        scores = lax.dot_general(
            q[:, columns], keys, (((1,), (1,)), ((), ())), preferred_element_type=jnp.float32
        ) * float(DEPTH) ** (-0.5)
        raised = jnp.exp(scores - jnp.max(scores, axis=1, keepdims=True))
        weights = (raised / jnp.sum(raised, axis=1, keepdims=True)).astype(jnp.bfloat16)
        att[:, columns] = jnp.dot(weights, values, preferred_element_type=jnp.float32).astype(jnp.bfloat16)

    locals_[2].wait()
    locals_[3].wait()
    wg.wait_siblings()

    width = wbuf.shape[3]

    def project(k, squares):
        columns = pl.ds(pl.multiple_of(k * width, width), width)
        part = jnp.dot(
            att[...], wbuf[k].reshape(-1, width), preferred_element_type=jnp.float32
        ) + res[:, columns].astype(jnp.float32)
        summed[:, columns] = part
        return squares + part * part

    squares = lax.fori_loop(0, GROUP, project, jnp.zeros((128, width), jnp.float32))
    mean = jnp.sum(squares, axis=1, keepdims=True) / summed.shape[1]
    scale = lax.rsqrt(mean + 1e-06)

    @pl.loop(0, GROUP)
    def _(k):
        columns = pl.ds(pl.multiple_of(k * width, width), width)
        hidden = (summed[:, columns] * scale * gain[:, columns]).astype(jnp.bfloat16)
        hbuf[me, :, :, columns] = hidden.reshape(2, 64, width)

    hg.wave1()
    locals_[4].wait()

    @pl.loop(1, GROUP)
    def _(j):
        other = (me + j) % GROUP
        pltpu.make_async_copy(idbuf.at[other], idbuf.at[other], id_recv.at[other]).wait()

    first_id = me * head.shape[0]
    vocab = lax.broadcasted_iota(jnp.int32, (head.shape[0], 128), 0) + first_id

    @pl.loop(0, 8)
    def _(step):
        @pl.when(step == 1)
        def _():
            hg.wave2()
            hg.wave3()

        @pl.when(step == 4)
        def _():
            hg.wave4()

        dx = jnp.where((step == 1) | (step > 4), 1, 0)
        turn = jnp.where(step > 4, step - 4, jnp.where(step > 1, step - 1, 0))
        dz = jnp.where(turn == 2, 3, jnp.where(turn == 3, 2, turn))
        chip = ((me // 8 + dx) % 2) * 4 + ((me // 2) % 4 + dz) % 4
        hg.wait_slot(2 * chip + hg.core % 2)
        tokens = hbuf[pl.ds(2 * chip, 2)].reshape(256, -1)
        logits[...] = lax.dot_general(
            head[...], tokens, (((1,), (1,)), ((), ())), preferred_element_type=jnp.float32
        )
        for c in range(2):
            slot = 2 * chip + c
            block = logits[:, c * 128 : (c + 1) * 128]
            largest = jnp.max(block, axis=0, keepdims=True)
            total = jnp.sum(jnp.exp(block - largest), axis=0, keepdims=True)
            picked = jnp.sum(jnp.where(vocab == idbuf[slot][0:1], block, 0.0), axis=0, keepdims=True)
            stat_out[slot, 0:1] = largest
            stat_out[slot, 1:2] = total
            stat_out[slot, 2:3] = picked
            stat_out[slot, 3:8] = jnp.zeros((5, 128), jnp.float32)

    @pl.loop(1, GROUP)
    def _(j):
        other = (me + j) % GROUP
        pltpu.make_async_remote_copy(
            src_ref=stat_out.at[other],
            dst_ref=stat_in.at[me],
            send_sem=stat_send,
            recv_sem=stat_recv.at[me],
            device_id={"fsdp": other},
            device_id_type=MESH,
        ).start()

    stat_in[me] = stat_out[me]

    @pl.loop(1, GROUP)
    def _(j):
        other = (me + j) % GROUP
        pltpu.make_async_copy(stat_in.at[other], stat_in.at[other], stat_recv.at[other]).wait()

    largest = stat_in[:, 0, :]
    highest = jnp.max(largest, axis=0, keepdims=True)
    total = jnp.sum(stat_in[:, 1, :] * jnp.exp(largest - highest), axis=0, keepdims=True)
    picked = jnp.sum(stat_in[:, 2, :], axis=0, keepdims=True)
    new = picked - (highest + jnp.log(total))
    position = (me % 2) * 128 + lax.broadcasted_iota(jnp.int32, (1, 128), 1)
    live = position < lengths[0, me // 2]
    before = old[...]
    ratio_out[...] = jnp.where(live, new - before, 0.0)
    gap = jnp.clip(before - new, -3.0, 3.0)
    kl_out[...] = jnp.where(live, jnp.exp(gap) - gap - 1.0, 0.0)

    wg.drain()
    hg.drain()
    dg.drain()
    for buf, count, sem in ((dbuf, 7, dp_send), (idbuf, 15, id_send), (stat_out, 15, stat_send)):
        view = buf.at[pl.ds(0, count)]
        pltpu.make_async_copy(view, view, sem).wait()


def on_device(
    queries, doc_kv, residual, out_weight, out_gain, head, source, lengths, sampled, old_logprob
):
    tokens, width = queries.shape
    columns = residual.shape[1]
    share = out_weight.shape[1]
    bf16, f32 = jnp.bfloat16, jnp.float32
    smem = pl.BlockSpec(memory_space=pltpu.SMEM)
    vmem = pl.BlockSpec(memory_space=pltpu.VMEM)
    any_ = pl.BlockSpec(memory_space=pl.ANY)
    dma = pltpu.SemaphoreType.DMA
    out = jax.ShapeDtypeStruct((1, tokens), f32)
    ratio, kl = pl.pallas_call(
        kernel,
        out_shape=(out, out),
        in_specs=[smem, smem, vmem, vmem, vmem] + [any_] * 5,
        out_specs=(vmem, vmem),
        scratch_shapes=[
            pltpu.VMEM(head.shape, bf16),
            pltpu.VMEM((GROUP, 2, width // 2, share), bf16),
            pltpu.VMEM((GROUP, 2, tokens // 2, columns), bf16),
            pltpu.VMEM((ROWS, 2, doc_kv.shape[2], width), bf16),
            pltpu.VMEM((GROUP, 2, doc_kv.shape[2], width), bf16),
            pltpu.VMEM((tokens, width), bf16),
            pltpu.VMEM((tokens, columns), bf16),
            pltpu.VMEM((tokens, width), bf16),
            pltpu.VMEM((tokens, columns), f32),
            pltpu.VMEM((head.shape[0], 256), f32),
            pltpu.VMEM((GROUP, 8, 128), jnp.int32),
            pltpu.VMEM((GROUP, 8, 128), f32),
            pltpu.VMEM((GROUP, 8, 128), f32),
            dma((5,)),
            dma,
            dma((GROUP, 2, PIECES)),
            dma,
            dma((GROUP, 2, PIECES)),
            dma,
            dma((GROUP, 2, 1)),
            dma,
            dma((ROWS,)),
            dma,
            dma((GROUP,)),
            dma,
            dma((GROUP,)),
        ],
        compiler_params=pltpu.CompilerParams(
            collective_id=0, has_side_effects=True, vmem_limit_bytes=60 * 1024 * 1024
        ),
    )(
        source,
        lengths,
        sampled.reshape(1, tokens),
        old_logprob.reshape(1, tokens),
        out_gain.reshape(1, columns),
        queries,
        doc_kv.reshape(2, doc_kv.shape[2], width),
        residual,
        out_weight.reshape(2, width // 2, share),
        head,
    )
    return ratio.reshape(tokens), kl.reshape(tokens)


def solution(mesh):
    return jax.shard_map(
        on_device,
        mesh=mesh,
        in_specs=(
            P(("dp", "fsdp"), None),
            P(None, "dp", "fsdp", None),
            P(("dp", "fsdp"), None),
            P(None, "fsdp"),
            P(),
            P("fsdp", None),
            P(),
            P("dp", None),
            P(("dp", "fsdp")),
            P(("dp", "fsdp")),
        ),
        out_specs=(P(("dp", "fsdp")), P(("dp", "fsdp"))),
        check_vma=False,
    )
```

time: 399 us -> 200 us (0.50)
  waiting for transfers between devices: 227 us -> 0 us
  Pallas kernels: 0 us -> 196 us
  blocking collectives: 71.7 us -> 0 us
  local copies, waits for them, and re-layouts: 38.8 us -> 2.25 us
  matrix products: 36.5 us -> 0 us
  between operations: 15.9 us -> 0.64 us
  other arithmetic: 6.93 us -> 0 us
    all_gather x4 -> x0, waiting for transfers between devices: 227 us -> none  [the longest x1 73.2 us: on_device(): lax.all_gather(hidden, 'fsdp', axis=0, tiled=True)]
    pallas_call x0 -> x1, Pallas kernels: none -> 196 us  [on_device(): pl.pallas_call(kernel, out_shape=(out, out), in_specs=[smem, smem, vmem,...]
    all_gather x4 -> x0, blocking collectives: 71.7 us -> none  [the longest x3 54 us: joined(): pieces = jax.tree.map(lambda part: lax.all_gather(part, axis), value)]
    dot_general x4 -> x0, matrix products: 36.5 us -> none  [the longest x1 22.8 us: on_device(): lax.dot_general(group_hidden, head, (((1,), (1,)), ((), ())), preferred_e...]
    slice x11 -> x0, local copies, waits for them, and re-layouts: 21.1 us -> none  [the longest x2 21 us: on_device(): attended = attend(queries, whole_doc[0], whole_doc[1], HEADS)]
    unnamed x20 -> x2, local copies, waits for them, and re-layouts: 13.4 us -> 2.25 us
    dynamic_slice x33 -> x0, local copies, waits for them, and re-layouts: 4.25 us -> none  [the longest x1 1.83 us: on_device(): lax.dynamic_index_in_dim(every_doc, source[row_pos], 1, keepdims=False)]
  transfers between devices with their start and end apart: 4 -> 0, of which waited for: 4 -> 0; matrix products, arithmetic and copies ran while one was open for 9% -> 0% of each run, Pallas kernels for 0% -> 0%
where the time goes in v1:
time: 200 us; the launch traced here: 198 us
  Pallas kernels  196 us (98%)
  local copies, waits for them, and re-layouts  2.25 us (1%)
    pallas_call x1, Pallas kernels, on_device(): pl.pallas_call(kernel, out_shape=(out, out), in_specs=[smem, smem, vmem,...  196 us

profile of v1, /device:TPU:1, one launch (start us, length us, event | category | flops | bytes accessed | tf_op | source)
XLA Modules:
  0.0 198.4 jit_solution(189717657208167525)
XLA Ops:
  0.6 195.5 %shard_map.113 = (f32[1,128]{1,0:T(1,128)}, f32[1,128]{1,0:T(1,128)}) custom-call(s32[8]{0:T(128)} %source.1, s32[1,8]{1,0:T(1,128)} %lengths.1, s32[1,128]{1,0:T(1,128)} %bitcast.10, f32[1,128]{1,0:T(1,128)} %bitcast.11, f32[1,4096]{1,0:T(1,128)} %bitcast.9, bf16[128,2048]{1,0:T(8,128)(2,1)} %q_hbm.1, bf16[2,32,2048]{2,1,0:T(8,128)(2,1)} %bitcast.8, ...), custom_call_target="tpu_custom_call" | custom-call | tf_op jit(solution)/shard_map/pallas_call | solution.py:371
  196.2 1.1 copy.14
  197.3 1.1 copy.15

commit v2 on v1

v2 whole, which is shorter than its diff:
```python
import jax
import jax.numpy as jnp
from jax import lax
from jax.experimental import pallas as pl
from jax.experimental.pallas import tpu as pltpu
from jax.sharding import PartitionSpec as P

HEADS = 8
DEPTH = 256
GROUP = 16
ROWS = 8
MESH = pl.DeviceIdType.MESH
PIECES = 4


class Gather:
    def __init__(self, me, buf, own, send_sem, recv_sem, pieces):
        self.me, self.buf, self.own = me, buf, own
        self.send_sem, self.recv_sem = send_sem, recv_sem
        self.pieces = pieces
        self.rows = buf.shape[2] // pieces
        x, z, core = me // 8, (me // 2) % 4, me % 2

        def slot(dx, dz):
            return ((x + dx) % 2) * 8 + ((z + dz) % 4) * 2 + core

        self.x, self.zp, self.zm, self.z2 = slot(1, 0), slot(0, 1), slot(0, 3), slot(0, 2)
        self.xzp, self.xzm, self.xz2 = slot(1, 1), slot(1, 3), slot(1, 2)
        self.core = me + 1 - 2 * core

    def at(self, ref, slot, half, p):
        return ref.at[slot, half, pl.ds(p * self.rows, self.rows)]

    def send(self, slot, half, p, *targets, own=False):
        dst = self.at(self.buf, slot, half, p)
        src = self.own.at[half, pl.ds(p * self.rows, self.rows)] if own else dst
        for target in targets:
            pltpu.make_async_remote_copy(
                src_ref=src,
                dst_ref=dst,
                send_sem=self.send_sem,
                recv_sem=self.recv_sem.at[slot, half, p],
                device_id={"fsdp": target},
                device_id_type=MESH,
            ).start()

    def wait(self, slot, half, p):
        view = self.at(self.buf, slot, half, p)
        pltpu.make_async_copy(view, view, self.recv_sem.at[slot, half, p]).wait()

    def each(self, step):
        if self.pieces == 1:
            step(0)
        else:
            pl.loop(0, self.pieces)(step)

    def wave1(self):
        def first(p):
            self.send(self.me, 0, p, self.x, own=True)
            self.send(self.me, 1, p, self.zp, self.zm, own=True)

        def second(p):
            self.send(self.me, 1, p, self.x, self.core, own=True)
            self.send(self.me, 0, p, self.zp, self.zm, self.core, own=True)

        self.each(first)
        self.each(second)

    def wave2(self):
        def step(p):
            self.wait(self.x, 0, p)
            self.send(self.x, 0, p, self.zp, self.zm, self.core)
            self.wait(self.zp, 1, p)
            self.send(self.zp, 1, p, self.zm, self.x, self.core)
            self.wait(self.zm, 1, p)
            self.send(self.zm, 1, p, self.x, self.core)

        self.each(step)

    def wave3(self):
        def step(p):
            self.wait(self.zm, 0, p)
            self.send(self.zm, 0, p, self.zp, self.core)
            self.wait(self.zp, 0, p)
            self.send(self.zp, 0, p, self.core)
            self.wait(self.x, 1, p)
            self.send(self.x, 1, p, self.core)

        def later(p):
            self.wait(self.z2, 1, p)
            self.send(self.z2, 1, p, self.x, self.core)
            self.wait(self.xzm, 0, p)
            self.send(self.xzm, 0, p, self.zp, self.core)
            self.wait(self.xzp, 0, p)
            self.send(self.xzp, 0, p, self.core)

        self.each(step)
        self.each(later)

    def wave4a(self):
        def step(p):
            for slot, half in ((self.xzp, 1), (self.xzm, 1)):
                self.wait(slot, half, p)
                self.send(slot, half, p, self.core)

        self.each(step)

    def wave4b(self):
        def step(p):
            for slot, half in ((self.z2, 0), (self.xz2, 0), (self.xz2, 1)):
                self.wait(slot, half, p)
                self.send(slot, half, p, self.core)

        self.each(step)

    def wait_slot(self, slot):
        for half in range(2):
            self.each(lambda p: self.wait(slot, half, p))

    def wait_siblings(self):
        other = self.core % 2

        @pl.loop(0, GROUP // 2)
        def _(k):
            self.wait_slot(2 * k + other)

    def drain(self):
        view = self.buf.at[pl.ds(0, 15)]
        pltpu.make_async_copy(view, view, self.send_sem).wait()


def kernel(
    source,
    lengths,
    ids,
    old,
    gain,
    q_hbm,
    doc_hbm,
    res_hbm,
    w_hbm,
    head_hbm,
    ratio_out,
    kl_out,
    head,
    wbuf,
    hbuf,
    dbuf,
    kv,
    qbuf,
    rbuf,
    att,
    summed,
    logits,
    idbuf,
    sq_out,
    sq_in,
    stat_out,
    stat_in,
    local_sems,
    head_sem,
    w_send,
    w_recv,
    h_send,
    h_recv,
    kv_send,
    kv_recv,
    dp_send,
    dp_recv,
    q_send,
    q_recv,
    r_send,
    r_recv,
    att_send,
    att_recv,
    sq_send,
    sq_recv,
    id_send,
    id_recv,
    stat_send,
    stat_recv,
):
    row = lax.axis_index("dp")
    me = lax.axis_index("fsdp")
    x, z, core = me // 8, (me // 2) % 4, me % 2
    xh, y = row // 4, row % 4
    quad = x * 2 + core
    share = wbuf.shape[3]
    tokens = qbuf.shape[1]

    def device(dx, dz, dc):
        return ((x + dx) % 2) * 8 + ((z + dz) % 4) * 2 + (core + dc) % 2

    def doc_row(dh, dy):
        return ((xh + dh) % 2) * 4 + (y + dy) % 4

    def columns_of(other, k):
        block = (other // 8) * 8 + k * 2 + other % 2
        return pl.ds(pl.multiple_of(block * share, share), share)

    def remote(src, dst, send, recv, **where):
        pltpu.make_async_remote_copy(
            src_ref=src, dst_ref=dst, send_sem=send, recv_sem=recv, device_id=where, device_id_type=MESH
        ).start()

    def arrived(view, sem):
        pltpu.make_async_copy(view, view, sem).wait()

    barrier = pltpu.get_barrier_semaphore()

    @pl.loop(1, GROUP)
    def _(j):
        pl.semaphore_signal(barrier, inc=1, device_id={"fsdp": (me + j) % GROUP}, device_id_type=MESH)

    near_rows = (doc_row(1, 0), doc_row(0, 1), doc_row(0, 3))
    for other in near_rows:
        pl.semaphore_signal(barrier, inc=1, device_id={"dp": other}, device_id_type=MESH)

    locals_ = [
        pltpu.make_async_copy(doc_hbm, dbuf.at[row], local_sems.at[0]),
        pltpu.make_async_copy(q_hbm, qbuf.at[x], local_sems.at[1]),
        pltpu.make_async_copy(w_hbm, wbuf.at[z], local_sems.at[2]),
    ] + [
        pltpu.make_async_copy(
            res_hbm.at[:, columns_of(me, k)],
            rbuf.at[quad, :, pl.ds(k * share, share)],
            local_sems.at[3 + k],
        )
        for k in range(4)
    ]
    for copy in locals_:
        copy.start()
    for k in range(GROUP):
        pltpu.make_async_copy(
            head_hbm.at[:, pl.ds(k * share, share)],
            head.at[(k // 8) * 2 + k % 2, :, pl.ds((k // 2) % 4 * share, share)],
            head_sem,
        ).start()
    idbuf[me] = jnp.broadcast_to(ids[...], (8, 128))

    pl.semaphore_wait(barrier, GROUP - 1 + 3)

    def send_doc(slot, halves, *targets, own=False):
        for half in halves:
            for target in targets:
                dst = dbuf.at[slot, half]
                remote(doc_hbm.at[half] if own else dst, dst, dp_send, dp_recv.at[slot, half], dp=target)

    def wait_doc(slot, half):
        arrived(dbuf.at[slot, half], dp_recv.at[slot, half])

    send_doc(row, (0, 1), *near_rows, own=True)
    remote(q_hbm, qbuf.at[x], q_send, q_recv, fsdp=device(1, 0, 0))

    w_rows = wbuf.shape[2] // PIECES

    def w_at(slot, half, p):
        return wbuf.at[slot, half, pl.ds(p * w_rows, w_rows)]

    def send_w(slot, half, p, *targets, own=False):
        dst = w_at(slot, half, p)
        src = w_hbm.at[half, pl.ds(p * w_rows, w_rows)] if own else dst
        for target in targets:
            remote(src, dst, w_send, w_recv.at[slot, half, p], fsdp=target)

    def wait_w(slot, half, p):
        arrived(w_at(slot, half, p), w_recv.at[slot, half, p])

    zp, zm = (z + 1) % 4, (z + 3) % 4

    @pl.loop(0, PIECES)
    def _(p):
        send_w(z, 0, p, device(0, 1, 0), own=True)
        send_w(z, 1, p, device(0, 3, 0), own=True)

    @pl.loop(0, PIECES)
    def _(p):
        send_w(z, 1, p, device(0, 1, 0), own=True)
        send_w(z, 0, p, device(0, 3, 0), own=True)

    partner, up, down = doc_row(1, 0), doc_row(0, 1), doc_row(0, 3)
    for half in range(2):
        wait_doc(partner, half)
        send_doc(partner, (half,), up, down)

    quad_peers = (device(1, 0, 0), device(0, 0, 1), device(1, 0, 1))
    for other in quad_peers:
        for k in range(4):
            remote(
                res_hbm.at[:, columns_of(other, k)],
                rbuf.at[quad, :, pl.ds(k * share, share)],
                r_send,
                r_recv.at[quad],
                fsdp=other,
            )

    @pl.loop(1, GROUP)
    def _(j):
        remote(idbuf.at[me], idbuf.at[me], id_send, id_recv.at[me], fsdp=(me + j) % GROUP)

    for dh in range(2):
        wait_doc(doc_row(dh, 3), 0)
        send_doc(doc_row(dh, 3), (0,), up)
        wait_doc(doc_row(dh, 1), 1)
        send_doc(doc_row(dh, 1), (1,), down)

    @pl.loop(0, PIECES)
    def _(p):
        wait_w(zm, 0, p)
        send_w(zm, 0, p, device(0, 1, 0))
        wait_w(zp, 1, p)
        send_w(zp, 1, p, device(0, 3, 0))

    for dh in range(2):
        wait_doc(doc_row(dh, 3), 1)
        wait_doc(doc_row(dh, 1), 0)
        for half in range(2):
            wait_doc(doc_row(dh, 2), half)
    locals_[0].wait()

    hg = Gather(me, hbuf, hbuf.at[me], h_send, h_recv, PIECES)
    dg = Gather(me, kv, kv.at[me], kv_send, kv_recv, 1)
    kv[me] = dbuf[source[row]]
    dg.wave1()
    dg.wave2()
    dg.wave3()
    dg.wave4a()
    dg.wave4b()
    dg.wait_siblings()

    locals_[1].wait()
    arrived(qbuf.at[1 - x], q_recv)

    @pl.loop(0, HEADS)
    def _(h):
        columns = pl.ds(pl.multiple_of(h * DEPTH, DEPTH), DEPTH)
        keys = kv[:, 0, :, columns].reshape(-1, DEPTH)
        values = kv[:, 1, :, columns].reshape(-1, DEPTH)
        scores = lax.dot_general(
            qbuf[:, :, columns].reshape(-1, DEPTH),
            keys,
            (((1,), (1,)), ((), ())),
            preferred_element_type=jnp.float32,
        ) * float(DEPTH) ** (-0.5)
        raised = jnp.exp(scores - jnp.max(scores, axis=1, keepdims=True))
        weights = (raised / jnp.sum(raised, axis=1, keepdims=True)).astype(jnp.bfloat16)
        mixed = jnp.dot(weights, values, preferred_element_type=jnp.float32).astype(jnp.bfloat16)
        att[core, :, :, columns] = mixed.reshape(2, tokens, DEPTH)

    remote(att.at[core], att.at[core], att_send, att_recv, fsdp=device(0, 0, 1))

    for copy in locals_[2:]:
        copy.wait()

    @pl.loop(0, PIECES)
    def _(p):
        wait_w(zp, 0, p)
        wait_w(zm, 1, p)
        wait_w((z + 2) % 4, 0, p)
        wait_w((z + 2) % 4, 1, p)

    for other in quad_peers:
        slot = (other // 8) * 2 + other % 2
        arrived(rbuf.at[slot], r_recv.at[slot])
    arrived(att.at[1 - core], att_recv)

    def project(k, squares):
        columns = pl.ds(pl.multiple_of(k * share, share), share)
        weight = wbuf[k].reshape(-1, share)
        both = [
            jnp.dot(att[c].reshape(2 * tokens, -1), weight, preferred_element_type=jnp.float32)
            for c in range(2)
        ]
        out = []
        for slot in range(4):
            mixed = both[slot % 2][(slot // 2) * tokens : (slot // 2 + 1) * tokens]
            part = mixed + rbuf[slot, :, columns].astype(jnp.float32)
            summed[slot, :, columns] = part
            out.append(squares[slot] + part * part)
        return tuple(out)

    zero = jnp.zeros((tokens, share), jnp.float32)
    squares = lax.fori_loop(0, 4, project, (zero,) * 4)
    for slot in range(4):
        own = jnp.sum(squares[slot], axis=1, keepdims=True)
        sq_out[slot] = jnp.broadcast_to(own, (tokens, 128)).T[0:8]
    for other in quad_peers:
        remote(sq_out, sq_in.at[quad], sq_send, sq_recv.at[quad], fsdp=other)
    sq_in[quad] = sq_out[...]
    for other in quad_peers:
        slot = (other // 8) * 2 + other % 2
        arrived(sq_in.at[slot], sq_recv.at[slot])
    mean = (sq_in[0] + sq_in[1] + sq_in[2] + sq_in[3]) / head_hbm.shape[1]
    scale = lax.rsqrt(mean + 1e-06)
    for slot in range(4):
        factor = jnp.broadcast_to(scale[slot, 0:1], (128, tokens)).T[:, 0:1]
        for k in range(4):
            columns = pl.ds(k * share, share)
            hidden = summed[slot, :, columns] * factor * gain[:, columns_of(me, k)]
            hbuf[me, slot // 2, pl.ds((slot % 2) * tokens, tokens), columns] = hidden.astype(jnp.bfloat16)

    hg.wave1()
    arrived(head, head_sem)

    @pl.loop(1, GROUP)
    def _(j):
        other = (me + j) % GROUP
        arrived(idbuf.at[other], id_recv.at[other])

    vocab = lax.broadcasted_iota(jnp.int32, (head.shape[1], 128), 0) + me * head.shape[1]

    @pl.loop(0, 8)
    def _(step):
        @pl.when(step == 0)
        def _():
            hg.wave2()

        @pl.when(step == 1)
        def _():
            hg.wave3()

        @pl.when(step == 4)
        def _():
            hg.wave4a()

        @pl.when(step == 6)
        def _():
            hg.wave4b()

        middle = (step >= 2) & (step < 6)
        half = jnp.where(middle, (step - 2) // 2, step % 2)
        dz = jnp.where(step < 2, 0, jnp.where(step >= 6, 2, 1 + 2 * (step % 2)))
        spot = (z + dz) % 4
        for dx in range(2):
            slot = dx * 8 + spot * 2 + 1 - core
            hg.each(lambda p: hg.wait(slot, half, p))
        total = None
        for k in range(4):
            slot = (k // 2) * 8 + spot * 2 + k % 2
            part = lax.dot_general(
                head[k], hbuf[slot, half], (((1,), (1,)), ((), ())), preferred_element_type=jnp.float32
            )
            total = part if total is None else total + part
        logits[...] = total
        for c in range(2):
            slot = half * 8 + spot * 2 + c
            block = logits[:, c * 128 : (c + 1) * 128]
            largest = jnp.max(block, axis=0, keepdims=True)
            total = jnp.sum(jnp.exp(block - largest), axis=0, keepdims=True)
            picked = jnp.sum(jnp.where(vocab == idbuf[slot][0:1], block, 0.0), axis=0, keepdims=True)
            stat_out[slot, 0:1] = largest
            stat_out[slot, 1:2] = total
            stat_out[slot, 2:3] = picked
            stat_out[slot, 3:8] = jnp.zeros((5, 128), jnp.float32)

    @pl.loop(1, GROUP)
    def _(j):
        other = (me + j) % GROUP
        remote(stat_out.at[other], stat_in.at[me], stat_send, stat_recv.at[me], fsdp=other)

    stat_in[me] = stat_out[me]

    @pl.loop(1, GROUP)
    def _(j):
        other = (me + j) % GROUP
        arrived(stat_in.at[other], stat_recv.at[other])

    largest = stat_in[:, 0, :]
    highest = jnp.max(largest, axis=0, keepdims=True)
    total = jnp.sum(stat_in[:, 1, :] * jnp.exp(largest - highest), axis=0, keepdims=True)
    picked = jnp.sum(stat_in[:, 2, :], axis=0, keepdims=True)
    new = picked - (highest + jnp.log(total))
    position = core * tokens + lax.broadcasted_iota(jnp.int32, (1, 128), 1)
    live = position < lengths[0, me // 2]
    before = old[...]
    ratio_out[...] = jnp.where(live, new - before, 0.0)
    gap = jnp.clip(before - new, -3.0, 3.0)
    kl_out[...] = jnp.where(live, jnp.exp(gap) - gap - 1.0, 0.0)

    hg.drain()
    dg.drain()
    for buf, count, sem in (
        (wbuf, 3, w_send),
        (dbuf, 7, dp_send),
        (rbuf, 3, r_send),
        (qbuf, 1, q_send),
        (att, 1, att_send),
        (sq_in, 3, sq_send),
        (idbuf, 15, id_send),
        (stat_out, 15, stat_send),
    ):
        view = buf.at[pl.ds(0, count)]
        arrived(view, sem)


def on_device(
    queries, doc_kv, residual, out_weight, out_gain, head, source, lengths, sampled, old_logprob
):
    tokens, width = queries.shape
    columns = residual.shape[1]
    share = out_weight.shape[1]
    positions = doc_kv.shape[2]
    bf16, f32 = jnp.bfloat16, jnp.float32
    smem = pl.BlockSpec(memory_space=pltpu.SMEM)
    vmem = pl.BlockSpec(memory_space=pltpu.VMEM)
    any_ = pl.BlockSpec(memory_space=pl.ANY)
    dma = pltpu.SemaphoreType.DMA
    out = jax.ShapeDtypeStruct((1, tokens), f32)
    ratio, kl = pl.pallas_call(
        kernel,
        out_shape=(out, out),
        in_specs=[smem, smem, vmem, vmem, vmem] + [any_] * 5,
        out_specs=(vmem, vmem),
        scratch_shapes=[
            pltpu.VMEM((4, head.shape[0], columns // 4), bf16),
            pltpu.VMEM((4, 2, width // 2, share), bf16),
            pltpu.VMEM((GROUP, 2, 2 * tokens, columns // 4), bf16),
            pltpu.VMEM((ROWS, 2, positions, width), bf16),
            pltpu.VMEM((GROUP, 2, positions, width), bf16),
            pltpu.VMEM((2, tokens, width), bf16),
            pltpu.VMEM((4, tokens, columns // 4), bf16),
            pltpu.VMEM((2, 2, tokens, width), bf16),
            pltpu.VMEM((4, tokens, columns // 4), f32),
            pltpu.VMEM((head.shape[0], 256), f32),
            pltpu.VMEM((GROUP, 8, 128), jnp.int32),
            pltpu.VMEM((4, 8, 128), f32),
            pltpu.VMEM((4, 4, 8, 128), f32),
            pltpu.VMEM((GROUP, 8, 128), f32),
            pltpu.VMEM((GROUP, 8, 128), f32),
            dma((7,)),
            dma,
            dma,
            dma((4, 2, PIECES)),
            dma,
            dma((GROUP, 2, PIECES)),
            dma,
            dma((GROUP, 2, 1)),
            dma,
            dma((ROWS, 2)),
            dma,
            dma,
            dma,
            dma((4,)),
            dma,
            dma,
            dma,
            dma((4,)),
            dma,
            dma((GROUP,)),
            dma,
            dma((GROUP,)),
        ],
        compiler_params=pltpu.CompilerParams(
            collective_id=0, has_side_effects=True, vmem_limit_bytes=60 * 1024 * 1024
        ),
    )(
        source,
        lengths,
        sampled.reshape(1, tokens),
        old_logprob.reshape(1, tokens),
        out_gain.reshape(1, columns),
        queries,
        doc_kv.reshape(2, positions, width),
        residual,
        out_weight.reshape(2, width // 2, share),
        head,
    )
    return ratio.reshape(tokens), kl.reshape(tokens)


def solution(mesh):
    return jax.shard_map(
        on_device,
        mesh=mesh,
        in_specs=(
            P(("dp", "fsdp"), None),
            P(None, "dp", "fsdp", None),
            P(("dp", "fsdp"), None),
            P(None, "fsdp"),
            P(),
            P("fsdp", None),
            P(),
            P("dp", None),
            P(("dp", "fsdp")),
            P(("dp", "fsdp")),
        ),
        out_specs=(P(("dp", "fsdp")), P(("dp", "fsdp"))),
        check_vma=False,
    )
```

time: 200 us -> 157 us (0.79)
  Pallas kernels: 196 us -> 154 us
    pallas_call x1, Pallas kernels: 196 us -> 154 us  [on_device(): pl.pallas_call(kernel, out_shape=(out, out), in_specs=[smem, smem, vmem,...]
where the time goes in v2:
time: 157 us
  Pallas kernels  154 us (98%)
  local copies, waits for them, and re-layouts  2.25 us (1%)
    pallas_call x1, Pallas kernels, on_device(): pl.pallas_call(kernel, out_shape=(out, out), in_specs=[smem, smem, vmem,...  154 us

profile of v2, /device:TPU:1, one launch (start us, length us, event | category | flops | bytes accessed | tf_op | source)
XLA Modules:
  0.0 157.1 jit_solution(3124029693241541391)
XLA Ops:
  0.6 154.2 %shard_map.113 = (f32[1,128]{1,0:T(1,128)}, f32[1,128]{1,0:T(1,128)}) custom-call(s32[8]{0:T(128)} %source.1, s32[1,8]{1,0:T(1,128)} %lengths.1, s32[1,128]{1,0:T(1,128)} %bitcast.10, f32[1,128]{1,0:T(1,128)} %bitcast.11, f32[1,4096]{1,0:T(1,128)} %bitcast.9, bf16[128,2048]{1,0:T(8,128)(2,1)} %q_hbm.1, bf16[2,32,2048]{2,1,0:T(8,128)(2,1)} %bitcast.8, ...), custom_call_target="tpu_custom_call" | custom-call | tf_op jit(solution)/shard_map/pallas_call | solution.py:509
  154.9 1.1 copy.14
  156.0 1.1 copy.15

commit v3 on v2

v3 whole, which is shorter than its diff:
```python
import jax
import jax.numpy as jnp
from jax import lax
from jax.experimental import pallas as pl
from jax.experimental.pallas import tpu as pltpu
from jax.sharding import PartitionSpec as P

HEADS = 8
DEPTH = 256
GROUP = 16
ROWS = 8
MESH = pl.DeviceIdType.MESH
PIECES = 4
HIDDEN = 16
VIA_X = 9


class Gather:
    def __init__(self, me, view, own, send_sem, recv_sem, first, second):
        self.me, self.view, self.own = me, view, own
        self.send_sem, self.recv_sem = send_sem, recv_sem
        self.first, self.second = first, second
        self.middle = (second[0] + second[1] + 1) // 2
        x, z, core = me // 8, (me // 2) % 4, me % 2

        def slot(dx, dz):
            return ((x + dx) % 2) * 8 + ((z + dz) % 4) * 2 + core

        self.x, self.zp, self.zm, self.z2 = slot(1, 0), slot(0, 1), slot(0, 3), slot(0, 2)
        self.xzp, self.xzm, self.xz2 = slot(1, 1), slot(1, 3), slot(1, 2)
        self.core = me + 1 - 2 * core

    def send(self, slot, p, *targets, own=False):
        dst = self.view(slot, p)
        src = self.own(p) if own else dst
        for target in targets:
            pltpu.make_async_remote_copy(
                src_ref=src,
                dst_ref=dst,
                send_sem=self.send_sem,
                recv_sem=self.recv_sem.at[slot, p],
                device_id={"fsdp": target},
                device_id_type=MESH,
            ).start()

    def wait(self, slot, p):
        view = self.view(slot, p)
        pltpu.make_async_copy(view, view, self.recv_sem.at[slot, p]).wait()

    def pass_on(self, slot, p, *targets):
        self.wait(slot, p)
        self.send(slot, p, *targets, self.core)

    def each(self, low, high, step):
        if high - low == 1:
            step(low)
        elif high > low:
            pl.loop(low, high)(step)

    def wave1(self):
        self.each(*self.first, lambda p: self.send(self.me, p, self.x, own=True))
        self.each(*self.second, lambda p: self.send(self.me, p, self.zp, self.zm, own=True))
        self.each(*self.first, lambda p: self.send(self.me, p, self.zp, self.zm, self.core, own=True))
        self.each(*self.second, lambda p: self.send(self.me, p, self.x, self.core, own=True))

    def wave2(self):
        self.each(*self.first, lambda p: self.pass_on(self.x, p, self.zp, self.zm))

    def wave3(self):
        def up(p):
            self.pass_on(self.zp, p, self.x)
            self.pass_on(self.zm, p, self.zp, self.x)

        def down(p):
            self.pass_on(self.zp, p, self.zm, self.x)
            self.pass_on(self.zm, p, self.x)

        def own_side(p):
            self.pass_on(self.zm, p, self.zp)
            self.pass_on(self.zp, p)

        self.each(self.middle, self.second[1], up)
        self.each(self.second[0], self.middle, down)
        self.each(*self.first, own_side)
        self.each(*self.second, lambda p: self.pass_on(self.x, p))

    def wave4(self):
        def far_side(p):
            self.pass_on(self.xzp, p, self.zm)
            self.pass_on(self.xzm, p)

        self.each(*self.first, far_side)

    def wave5(self):
        def far_side(p):
            self.pass_on(self.xzp, p)
            self.pass_on(self.xzm, p)

        self.each(*self.second, lambda p: self.pass_on(self.z2, p, self.x))
        self.each(*self.second, far_side)

    def last(self, low, high):
        def step(p):
            self.pass_on(self.z2, p)
            self.pass_on(self.xz2, p)

        self.each(max(low, self.first[0]), min(high, self.first[1]), step)
        self.each(
            max(low, self.second[0]), min(high, self.second[1]), lambda p: self.pass_on(self.xz2, p)
        )


def kernel(
    source,
    lengths,
    ids,
    old,
    gain,
    q_hbm,
    doc_hbm,
    res_hbm,
    w_hbm,
    head_hbm,
    ratio_out,
    kl_out,
    head,
    wbuf,
    hbuf,
    dbuf,
    kv,
    qbuf,
    rbuf,
    att,
    summed,
    logits,
    idbuf,
    sq_out,
    sq_in,
    stat_out,
    stat_in,
    local_sems,
    head_sem,
    w_send,
    w_recv,
    h_send,
    h_recv,
    kv_send,
    kv_recv,
    dp_send,
    dp_recv,
    q_send,
    q_recv,
    r_send,
    r_recv,
    att_send,
    att_recv,
    sq_send,
    sq_recv,
    id_send,
    id_recv,
    stat_send,
    stat_recv,
):
    row = lax.axis_index("dp")
    me = lax.axis_index("fsdp")
    x, z, core = me // 8, (me // 2) % 4, me % 2
    xh, y = row // 4, row % 4
    quad = x * 2 + core
    share = wbuf.shape[3]
    tokens = qbuf.shape[1]

    def device(dx, dz, dc):
        return ((x + dx) % 2) * 8 + ((z + dz) % 4) * 2 + (core + dc) % 2

    def doc_row(dh, dy):
        return ((xh + dh) % 2) * 4 + (y + dy) % 4

    def columns_of(other, k):
        block = (other // 8) * 8 + k * 2 + other % 2
        return pl.ds(pl.multiple_of(block * share, share), share)

    def remote(src, dst, send, recv, **where):
        pltpu.make_async_remote_copy(
            src_ref=src, dst_ref=dst, send_sem=send, recv_sem=recv, device_id=where, device_id_type=MESH
        ).start()

    def arrived(view, sem):
        pltpu.make_async_copy(view, view, sem).wait()

    barrier = pltpu.get_barrier_semaphore()

    @pl.loop(1, GROUP)
    def _(j):
        pl.semaphore_signal(barrier, inc=1, device_id={"fsdp": (me + j) % GROUP}, device_id_type=MESH)

    near_rows = (doc_row(1, 0), doc_row(0, 1), doc_row(0, 3))
    for other in near_rows:
        pl.semaphore_signal(barrier, inc=1, device_id={"dp": other}, device_id_type=MESH)

    locals_ = [
        pltpu.make_async_copy(doc_hbm, dbuf.at[row], local_sems.at[0]),
        pltpu.make_async_copy(q_hbm, qbuf.at[x], local_sems.at[1]),
        pltpu.make_async_copy(w_hbm, wbuf.at[z], local_sems.at[2]),
    ] + [
        pltpu.make_async_copy(
            res_hbm.at[:, columns_of(me, k)],
            rbuf.at[quad, :, pl.ds(k * share, share)],
            local_sems.at[3 + k],
        )
        for k in range(4)
    ]
    for copy in locals_:
        copy.start()
    for k in range(GROUP):
        pltpu.make_async_copy(
            head_hbm.at[:, pl.ds(k * share, share)],
            head.at[:, pl.ds(((k // 8 * 2 + k % 2) * 4 + k // 2 % 4) * share, share)],
            head_sem,
        ).start()
    idbuf[me] = jnp.broadcast_to(ids[...], (8, 128))

    pl.semaphore_wait(barrier, GROUP - 1 + 3)

    def send_doc(slot, halves, *targets, own=False):
        for half in halves:
            for target in targets:
                dst = dbuf.at[slot, half]
                remote(doc_hbm.at[half] if own else dst, dst, dp_send, dp_recv.at[slot, half], dp=target)

    def wait_doc(slot, half):
        arrived(dbuf.at[slot, half], dp_recv.at[slot, half])

    send_doc(row, (0, 1), *near_rows, own=True)

    quad_peers = (device(1, 0, 0), device(0, 0, 1), device(1, 0, 1))
    remote(q_hbm, qbuf.at[x], q_send, q_recv, fsdp=device(1, 0, 0))

    w_rows = wbuf.shape[2] // PIECES

    def w_at(slot, half, p):
        return wbuf.at[slot, half, pl.ds(p * w_rows, w_rows)]

    def send_w(slot, half, p, *targets, own=False):
        dst = w_at(slot, half, p)
        src = w_hbm.at[half, pl.ds(p * w_rows, w_rows)] if own else dst
        for target in targets:
            remote(src, dst, w_send, w_recv.at[slot, half, p], fsdp=target)

    def wait_w(slot, half, p):
        arrived(w_at(slot, half, p), w_recv.at[slot, half, p])

    zp, zm = (z + 1) % 4, (z + 3) % 4

    @pl.loop(0, PIECES)
    def _(p):
        send_w(z, 0, p, device(0, 1, 0), own=True)
        send_w(z, 1, p, device(0, 3, 0), own=True)

    partner, up, down = doc_row(1, 0), doc_row(0, 1), doc_row(0, 3)
    for half in range(2):
        wait_doc(partner, half)
        send_doc(partner, (half,), up, down)

    for dh in range(2):
        wait_doc(doc_row(dh, 3), 0)
        send_doc(doc_row(dh, 3), (0,), up)
        wait_doc(doc_row(dh, 1), 1)
        send_doc(doc_row(dh, 1), (1,), down)

    @pl.loop(0, PIECES)
    def _(p):
        wait_w(zm, 0, p)
        send_w(zm, 0, p, device(0, 1, 0))
        wait_w(zp, 1, p)
        send_w(zp, 1, p, device(0, 3, 0))

    for dh in range(2):
        wait_doc(doc_row(dh, 3), 1)
        wait_doc(doc_row(dh, 1), 0)
        for half in range(2):
            wait_doc(doc_row(dh, 2), half)
    locals_[0].wait()

    half_width = kv.shape[3]
    for g in range(2):
        for half in range(2):
            kv[me, half * 2 + g] = dbuf[source[row], half, :, g * half_width : (g + 1) * half_width]

    def kv_view(slot, p):
        return kv.at[slot, p]

    groups = []
    for g in range(2):
        groups.append(
            Gather(me, kv_view, lambda p: kv.at[me, p], kv_send, kv_recv, (g, g + 1), (2 + g, 3 + g))
        )
    for group in groups:
        group.wave1()
    for wave in (Gather.wave2, Gather.wave3, Gather.wave4, Gather.wave5):
        for group in groups:
            wave(group)
    for other in quad_peers:
        for k in range(4):
            remote(
                res_hbm.at[:, columns_of(other, k)],
                rbuf.at[quad, :, pl.ds(k * share, share)],
                r_send,
                r_recv.at[quad],
                fsdp=other,
            )

    @pl.loop(1, GROUP)
    def _(j):
        remote(idbuf.at[me], idbuf.at[me], id_send, id_recv.at[me], fsdp=(me + j) % GROUP)


    @pl.loop(0, PIECES)
    def _(p):
        send_w(z, 1, p, device(0, 1, 0), own=True)
        send_w(z, 0, p, device(0, 3, 0), own=True)

    locals_[1].wait()
    arrived(qbuf.at[1 - x], q_recv)

    for g in range(2):
        groups[g].last(0, 4)

        @pl.loop(0, GROUP // 2)
        def _(k):
            for half in range(2):
                groups[g].wait(2 * k + 1 - core, half * 2 + g)

        @pl.loop(0, HEADS // 2, unroll=4)
        def _(h):
            columns = pl.ds(pl.multiple_of(h * DEPTH, DEPTH), DEPTH)
            whole = pl.ds(pl.multiple_of(h * DEPTH + g * half_width, DEPTH), DEPTH)
            keys = kv[:, g, :, columns].reshape(-1, DEPTH)
            values = kv[:, 2 + g, :, columns].reshape(-1, DEPTH)
            scores = lax.dot_general(
                qbuf[:, :, whole].reshape(-1, DEPTH),
                keys,
                (((1,), (1,)), ((), ())),
                preferred_element_type=jnp.float32,
            ) * float(DEPTH) ** (-0.5)
            raised = jnp.exp(scores - jnp.max(scores, axis=1, keepdims=True))
            weights = (raised / jnp.sum(raised, axis=1, keepdims=True)).astype(jnp.bfloat16)
            mixed = jnp.dot(weights, values, preferred_element_type=jnp.float32).astype(jnp.bfloat16)
            att[core, :, :, whole] = mixed.reshape(2, tokens, DEPTH)

        done = att.at[core, :, :, pl.ds(g * half_width, half_width)]
        remote(done, done, att_send, att_recv.at[g], fsdp=device(0, 0, 1))

    for copy in locals_[2:]:
        copy.wait()

    @pl.loop(0, PIECES)
    def _(p):
        wait_w(zp, 0, p)
        wait_w(zm, 1, p)
        wait_w((z + 2) % 4, 0, p)
        wait_w((z + 2) % 4, 1, p)

    for other in quad_peers:
        slot = (other // 8) * 2 + other % 2
        arrived(rbuf.at[slot], r_recv.at[slot])
    for g in range(2):
        arrived(att.at[1 - core, :, :, pl.ds(g * half_width, half_width)], att_recv.at[g])

    def project(k, squares):
        columns = pl.ds(pl.multiple_of(k * share, share), share)
        weight = wbuf[k].reshape(-1, share)
        mixed = jnp.dot(att[...].reshape(4 * tokens, -1), weight, preferred_element_type=jnp.float32)
        out = []
        for slot in range(4):
            start = ((slot % 2) * 2 + slot // 2) * tokens
            part = mixed[start : start + tokens] + rbuf[slot, :, columns].astype(jnp.float32)
            summed[slot, :, columns] = part
            out.append(squares[slot] + part * part)
        return tuple(out)

    zero = jnp.zeros((tokens, share), jnp.float32)
    squares = lax.fori_loop(0, 4, project, (zero,) * 4)
    for slot in range(4):
        own = jnp.sum(squares[slot], axis=1, keepdims=True)
        sq_out[slot] = jnp.broadcast_to(own, (tokens, 128)).T[0:8]
    for other in quad_peers:
        remote(sq_out, sq_in.at[quad], sq_send, sq_recv.at[quad], fsdp=other)
    sq_in[quad] = sq_out[...]
    for other in quad_peers:
        slot = (other // 8) * 2 + other % 2
        arrived(sq_in.at[slot], sq_recv.at[slot])
    mean = (sq_in[0] + sq_in[1] + sq_in[2] + sq_in[3]) / head_hbm.shape[1]
    scale = lax.rsqrt(mean + 1e-06)
    for slot in range(4):
        factor = jnp.broadcast_to(scale[slot, 0:1], (128, tokens)).T[:, 0:1]
        for k in range(4):
            columns = pl.ds(k * share, share)
            hidden = summed[slot, :, columns] * factor * gain[:, columns_of(me, k)]
            spot = pl.ds(pl.multiple_of((quad * 4 + k) * share, share), share)
            rows = pl.ds((slot // 2) * 2 * tokens + (slot % 2) * tokens, tokens)
            hbuf[z, rows, spot] = hidden.astype(jnp.bfloat16)

    piece = hbuf.shape[1] // HIDDEN
    quarter = hbuf.shape[2] // 4

    def hidden_view(slot, p):
        place = (slot // 8) * 2 + slot % 2
        return hbuf.at[
            (slot // 2) % 4,
            pl.ds(p * piece, piece),
            pl.ds(pl.multiple_of(place * quarter, quarter), quarter),
        ]

    hg = Gather(
        me, hidden_view, lambda p: hidden_view(me, p), h_send, h_recv, (0, VIA_X), (VIA_X, HIDDEN)
    )
    hg.wave1()
    arrived(head, head_sem)

    @pl.loop(1, GROUP)
    def _(j):
        other = (me + j) % GROUP
        arrived(idbuf.at[other], id_recv.at[other])

    vocab = lax.broadcasted_iota(jnp.int32, (head.shape[0], 128), 0) + me * head.shape[0]

    parts = HIDDEN // 4

    def finish(spot, start, count):
        rows = pl.ds(start, count * tokens)
        logits[:, : count * tokens] = lax.dot_general(
            head[...], hbuf[spot, rows], (((1,), (1,)), ((), ())), preferred_element_type=jnp.float32
        )
        for c in range(count):
            index = start // tokens + c
            slot = (index // 2) * 8 + spot * 2 + index % 2
            block = logits[:, c * tokens : (c + 1) * tokens]
            largest = jnp.max(block, axis=0, keepdims=True)
            total = jnp.sum(jnp.exp(block - largest), axis=0, keepdims=True)
            picked = jnp.sum(jnp.where(vocab == idbuf[slot][0:1], block, 0.0), axis=0, keepdims=True)
            stat_out[slot, 0:1] = largest
            stat_out[slot, 1:2] = total
            stat_out[slot, 2:3] = picked
            stat_out[slot, 3:8] = jnp.zeros((5, tokens), jnp.float32)

            @pl.when(slot != me)
            def _():
                remote(stat_out.at[slot], stat_in.at[me], stat_send, stat_recv.at[me], fsdp=slot)

    def wait_other_core(spot, low, high):
        for dx in range(2):
            slot = dx * 8 + spot * 2 + 1 - core
            pl.loop(low, high)(lambda p: hg.wait(slot, p))

    @pl.loop(0, 6)
    def _(step):
        for when, wave in ((0, hg.wave2), (1, hg.wave3), (2, hg.wave4), (4, hg.wave5)):
            pl.when(step == when)(wave)
        half = jnp.where(step < 2, step, (step - 2) // 2)
        dz = jnp.where(step < 2, 0, 1 + 2 * (step % 2))
        spot = (z + dz) % 4
        wait_other_core(spot, half * 2 * parts, half * 2 * parts + 2 * parts)
        finish(spot, half * 2 * tokens, 2)

    def last_quarter(step):
        quarter_of = (step % 2) * 2 + step // 2
        for k in range(4):
            pl.when(quarter_of == k)(lambda: hg.last(k * parts, (k + 1) * parts))
        wait_other_core(spot, quarter_of * parts, quarter_of * parts + parts)
        finish(spot, quarter_of * tokens, 1)

    spot = (z + 2) % 4
    pl.loop(0, 4)(last_quarter)

    stat_in[me] = stat_out[me]

    @pl.loop(1, GROUP)
    def _(j):
        other = (me + j) % GROUP
        arrived(stat_in.at[other], stat_recv.at[other])

    largest = stat_in[:, 0, :]
    highest = jnp.max(largest, axis=0, keepdims=True)
    total = jnp.sum(stat_in[:, 1, :] * jnp.exp(largest - highest), axis=0, keepdims=True)
    picked = jnp.sum(stat_in[:, 2, :], axis=0, keepdims=True)
    new = picked - (highest + jnp.log(total))
    position = core * tokens + lax.broadcasted_iota(jnp.int32, (1, 128), 1)
    live = position < lengths[0, me // 2]
    before = old[...]
    ratio_out[...] = jnp.where(live, new - before, 0.0)
    gap = jnp.clip(before - new, -3.0, 3.0)
    kl_out[...] = jnp.where(live, jnp.exp(gap) - gap - 1.0, 0.0)

    arrived(hbuf.at[:, pl.ds(0, 15 * hbuf.shape[1] // 16)], h_send)
    for buf, count, sem in (
        (kv, 15, kv_send),
        (wbuf, 3, w_send),
        (dbuf, 7, dp_send),
        (rbuf, 3, r_send),
        (qbuf, 1, q_send),
        (att, 1, att_send),
        (sq_in, 3, sq_send),
        (idbuf, 15, id_send),
        (stat_out, 15, stat_send),
    ):
        view = buf.at[pl.ds(0, count)]
        arrived(view, sem)


def on_device(
    queries, doc_kv, residual, out_weight, out_gain, head, source, lengths, sampled, old_logprob
):
    tokens, width = queries.shape
    columns = residual.shape[1]
    share = out_weight.shape[1]
    positions = doc_kv.shape[2]
    bf16, f32 = jnp.bfloat16, jnp.float32
    smem = pl.BlockSpec(memory_space=pltpu.SMEM)
    vmem = pl.BlockSpec(memory_space=pltpu.VMEM)
    any_ = pl.BlockSpec(memory_space=pl.ANY)
    dma = pltpu.SemaphoreType.DMA
    out = jax.ShapeDtypeStruct((1, tokens), f32)
    ratio, kl = pl.pallas_call(
        kernel,
        out_shape=(out, out),
        in_specs=[smem, smem, vmem, vmem, vmem] + [any_] * 5,
        out_specs=(vmem, vmem),
        scratch_shapes=[
            pltpu.VMEM(head.shape, bf16),
            pltpu.VMEM((4, 2, width // 2, share), bf16),
            pltpu.VMEM((4, 4 * tokens, columns), bf16),
            pltpu.VMEM((ROWS, 2, positions, width), bf16),
            pltpu.VMEM((GROUP, 4, positions, width // 2), bf16),
            pltpu.VMEM((2, tokens, width), bf16),
            pltpu.VMEM((4, tokens, columns // 4), bf16),
            pltpu.VMEM((2, 2, tokens, width), bf16),
            pltpu.VMEM((4, tokens, columns // 4), f32),
            pltpu.VMEM((head.shape[0], 256), f32),
            pltpu.VMEM((GROUP, 8, 128), jnp.int32),
            pltpu.VMEM((4, 8, 128), f32),
            pltpu.VMEM((4, 4, 8, 128), f32),
            pltpu.VMEM((GROUP, 8, 128), f32),
            pltpu.VMEM((GROUP, 8, 128), f32),
            dma((7,)),
            dma,
            dma,
            dma((4, 2, PIECES)),
            dma,
            dma((GROUP, HIDDEN)),
            dma,
            dma((GROUP, 4)),
            dma,
            dma((ROWS, 2)),
            dma,
            dma,
            dma,
            dma((4,)),
            dma,
            dma((2,)),
            dma,
            dma((4,)),
            dma,
            dma((GROUP,)),
            dma,
            dma((GROUP,)),
        ],
        compiler_params=pltpu.CompilerParams(
            collective_id=0, has_side_effects=True, vmem_limit_bytes=60 * 1024 * 1024
        ),
    )(
        source,
        lengths,
        sampled.reshape(1, tokens),
        old_logprob.reshape(1, tokens),
        out_gain.reshape(1, columns),
        queries,
        doc_kv.reshape(2, positions, width),
        residual,
        out_weight.reshape(2, width // 2, share),
        head,
    )
    return ratio.reshape(tokens), kl.reshape(tokens)


def solution(mesh):
    return jax.shard_map(
        on_device,
        mesh=mesh,
        in_specs=(
            P(("dp", "fsdp"), None),
            P(None, "dp", "fsdp", None),
            P(("dp", "fsdp"), None),
            P(None, "fsdp"),
            P(),
            P("fsdp", None),
            P(),
            P("dp", None),
            P(("dp", "fsdp")),
            P(("dp", "fsdp")),
        ),
        out_specs=(P(("dp", "fsdp")), P(("dp", "fsdp"))),
        check_vma=False,
    )
```

time: 157 us -> 144 us (0.917); the launches traced: 157 us -> 142 us
  Pallas kernels: 154 us -> 140 us
    pallas_call x1, Pallas kernels: 154 us -> 140 us  [on_device(): pl.pallas_call(kernel, out_shape=(out, out), in_specs=[smem, smem, vmem,...]
where the time goes in v3:
time: 144 us; the launch traced here: 142 us
  Pallas kernels  140 us (97%)
  local copies, waits for them, and re-layouts  2.25 us (2%)
    pallas_call x1, Pallas kernels, on_device(): pl.pallas_call(kernel, out_shape=(out, out), in_specs=[smem, smem, vmem,...  140 us

profile of v3, /device:TPU:1, one launch (start us, length us, event | category | flops | bytes accessed | tf_op | source)
XLA Modules:
  0.0 142.4 jit_solution(12514544997833400007)
XLA Ops:
  0.6 139.5 %shard_map.113 = (f32[1,128]{1,0:T(1,128)}, f32[1,128]{1,0:T(1,128)}) custom-call(s32[8]{0:T(128)} %source.1, s32[1,8]{1,0:T(1,128)} %lengths.1, s32[1,128]{1,0:T(1,128)} %bitcast.10, f32[1,128]{1,0:T(1,128)} %bitcast.11, f32[1,4096]{1,0:T(1,128)} %bitcast.9, bf16[128,2048]{1,0:T(8,128)(2,1)} %q_hbm.1, bf16[2,32,2048]{2,1,0:T(8,128)(2,1)} %bitcast.8, ...), custom_call_target="tpu_custom_call" | custom-call | tf_op jit(solution)/shard_map/pallas_call | solution.py:523
  140.2 1.1 copy.14
  141.3 1.1 copy.15

commit v4 on v3

--- a/solution.py
+++ b/solution.py
@@ -57,11 +57,13 @@
         elif high > low:
             pl.loop(low, high)(step)
 
-    def wave1(self):
-        self.each(*self.first, lambda p: self.send(self.me, p, self.x, own=True))
-        self.each(*self.second, lambda p: self.send(self.me, p, self.zp, self.zm, own=True))
-        self.each(*self.first, lambda p: self.send(self.me, p, self.zp, self.zm, self.core, own=True))
-        self.each(*self.second, lambda p: self.send(self.me, p, self.x, self.core, own=True))
+    def wave1(self, low=0, high=1 << 10):
+        first = max(low, self.first[0]), min(high, self.first[1])
+        second = max(low, self.second[0]), min(high, self.second[1])
+        self.each(*first, lambda p: self.send(self.me, p, self.x, own=True))
+        self.each(*second, lambda p: self.send(self.me, p, self.zp, self.zm, own=True))
+        self.each(*first, lambda p: self.send(self.me, p, self.zp, self.zm, self.core, own=True))
+        self.each(*second, lambda p: self.send(self.me, p, self.x, self.core, own=True))
 
     def wave2(self):
         self.each(*self.first, lambda p: self.pass_on(self.x, p, self.zp, self.zm))
@@ -126,7 +128,8 @@
     head,
     wbuf,
     hbuf,
-    dbuf,
+    doc_a,
+    doc_b,
     kv,
     qbuf,
     rbuf,
@@ -142,6 +145,8 @@
     head_sem,
     w_send,
     w_recv,
+    ws_send,
+    ws_recv,
     h_send,
     h_recv,
     kv_send,
@@ -197,19 +202,29 @@
     for other in near_rows:
         pl.semaphore_signal(barrier, inc=1, device_id={"dp": other}, device_id_type=MESH)
 
+    half_width = kv.shape[3]
+
+    def doc_piece(p):
+        return doc_hbm.at[p % 2, :, pl.ds(p // 2 * half_width, half_width)]
+
+    def doc_view(slot, p):
+        return (doc_a, doc_b)[p // 2].at[slot, p % 2]
+
     locals_ = [
-        pltpu.make_async_copy(doc_hbm, dbuf.at[row], local_sems.at[0]),
-        pltpu.make_async_copy(q_hbm, qbuf.at[x], local_sems.at[1]),
-        pltpu.make_async_copy(w_hbm, wbuf.at[z], local_sems.at[2]),
+        pltpu.make_async_copy(q_hbm, qbuf.at[x], local_sems.at[0]),
+        pltpu.make_async_copy(w_hbm, wbuf.at[z], local_sems.at[1]),
     ] + [
         pltpu.make_async_copy(
             res_hbm.at[:, columns_of(me, k)],
             rbuf.at[quad, :, pl.ds(k * share, share)],
-            local_sems.at[3 + k],
+            local_sems.at[2 + k],
         )
         for k in range(4)
     ]
-    for copy in locals_:
+    doc_locals = [
+        pltpu.make_async_copy(doc_piece(p), doc_view(row, p), local_sems.at[6 + p]) for p in range(4)
+    ]
+    for copy in doc_locals + locals_:
         copy.start()
     for k in range(GROUP):
         pltpu.make_async_copy(
@@ -221,70 +236,76 @@
 
     pl.semaphore_wait(barrier, GROUP - 1 + 3)
 
-    def send_doc(slot, halves, *targets, own=False):
-        for half in halves:
-            for target in targets:
-                dst = dbuf.at[slot, half]
-                remote(doc_hbm.at[half] if own else dst, dst, dp_send, dp_recv.at[slot, half], dp=target)
-
-    def wait_doc(slot, half):
-        arrived(dbuf.at[slot, half], dp_recv.at[slot, half])
-
-    send_doc(row, (0, 1), *near_rows, own=True)
-
     quad_peers = (device(1, 0, 0), device(0, 0, 1), device(1, 0, 1))
+    partner, up, down = near_rows
+
+    def send_row(view, sems, slot, p, *targets, src=None):
+        dst = view(slot, p)
+        for target in targets:
+            remote(dst if src is None else src, dst, sems[0], sems[1].at[slot, p], dp=target)
+
+    def wait_row(view, sems, slot, p):
+        arrived(view(slot, p), sems[1].at[slot, p])
+
+    def relay(view, sems, low, high):
+        for dh in range(2):
+            wait_row(view, sems, doc_row(dh, 3), low)
+            send_row(view, sems, doc_row(dh, 3), low, up)
+            wait_row(view, sems, doc_row(dh, 1), high)
+            send_row(view, sems, doc_row(dh, 1), high, down)
+
+    def wait_rest(view, sems, low, high):
+        for dh in range(2):
+            wait_row(view, sems, doc_row(dh, 3), high)
+            wait_row(view, sems, doc_row(dh, 1), low)
+            wait_row(view, sems, doc_row(dh, 2), low)
+            wait_row(view, sems, doc_row(dh, 2), high)
+
+    doc = (doc_view, (dp_send, dp_recv))
+
+    for p in range(4):
+        send_row(*doc, row, p, partner, up, down, src=doc_piece(p))
     remote(q_hbm, qbuf.at[x], q_send, q_recv, fsdp=device(1, 0, 0))
 
     w_rows = wbuf.shape[2] // PIECES
-
-    def w_at(slot, half, p):
-        return wbuf.at[slot, half, pl.ds(p * w_rows, w_rows)]
-
-    def send_w(slot, half, p, *targets, own=False):
-        dst = w_at(slot, half, p)
-        src = w_hbm.at[half, pl.ds(p * w_rows, w_rows)] if own else dst
-        for target in targets:
-            remote(src, dst, w_send, w_recv.at[slot, half, p], fsdp=target)
-
-    def wait_w(slot, half, p):
-        arrived(w_at(slot, half, p), w_recv.at[slot, half, p])
-
-    zp, zm = (z + 1) % 4, (z + 3) % 4
+    eighth = wbuf.shape[2] // 8
+    above, far, below = (z + 1) % 4, (z + 2) % 4, (z + 3) % 4
+
+    def send_w(half, p, target):
+        rows = pl.ds(p * w_rows, w_rows)
+        remote(
+            w_hbm.at[half, rows], wbuf.at[z, half, rows], w_send, w_recv.at[half, p], fsdp=target
+        )
+
+    def part_view(slot, p):
+        owner = (far, far, below, above)[p]
+        return wbuf.at[owner, (0, 1, 1, 0)[p], pl.ds(slot * eighth, eighth)]
+
+    part = (part_view, (ws_send, ws_recv))
+
+    for p in range(4):
+        rows = pl.ds(row * eighth, eighth)
+        half = (0, 1, 1, 0)[p]
+        remote(
+            w_hbm.at[half, rows],
+            wbuf.at[z, half, rows],
+            ws_send,
+            ws_recv.at[row, p],
+            fsdp=device(0, (2, 2, 1, 3)[p], 0),
+        )
 
     @pl.loop(0, PIECES)
     def _(p):
-        send_w(z, 0, p, device(0, 1, 0), own=True)
-        send_w(z, 1, p, device(0, 3, 0), own=True)
-
-    partner, up, down = doc_row(1, 0), doc_row(0, 1), doc_row(0, 3)
-    for half in range(2):
-        wait_doc(partner, half)
-        send_doc(partner, (half,), up, down)
-
-    for dh in range(2):
-        wait_doc(doc_row(dh, 3), 0)
-        send_doc(doc_row(dh, 3), (0,), up)
-        wait_doc(doc_row(dh, 1), 1)
-        send_doc(doc_row(dh, 1), (1,), down)
-
-    @pl.loop(0, PIECES)
-    def _(p):
-        wait_w(zm, 0, p)
-        send_w(zm, 0, p, device(0, 1, 0))
-        wait_w(zp, 1, p)
-        send_w(zp, 1, p, device(0, 3, 0))
-
-    for dh in range(2):
-        wait_doc(doc_row(dh, 3), 1)
-        wait_doc(doc_row(dh, 1), 0)
-        for half in range(2):
-            wait_doc(doc_row(dh, 2), half)
-    locals_[0].wait()
-
-    half_width = kv.shape[3]
-    for g in range(2):
-        for half in range(2):
-            kv[me, half * 2 + g] = dbuf[source[row], half, :, g * half_width : (g + 1) * half_width]
+        send_w(0, p, device(0, 1, 0))
+        send_w(1, p, device(0, 3, 0))
+
+    for p in (0, 1):
+        wait_row(*doc, partner, p)
+        send_row(*doc, partner, p, up, down)
+    relay(*doc, 0, 1)
+    for p in (2, 3):
+        wait_row(*doc, partner, p)
+        send_row(*doc, partner, p, up, down)
 
     def kv_view(slot, p):
         return kv.at[slot, p]
@@ -292,50 +313,38 @@
     groups = []
     for g in range(2):
         groups.append(
-            Gather(me, kv_view, lambda p: kv.at[me, p], kv_send, kv_recv, (g, g + 1), (2 + g, 3 + g))
+            Gather(
+                me,
+                kv_view,
+                lambda p: kv.at[me, p],
+                kv_send,
+                kv_recv,
+                (2 * g, 2 * g + 2),
+                (2 * g + 2, 2 * g + 2),
+            )
         )
-    for group in groups:
-        group.wave1()
-    for wave in (Gather.wave2, Gather.wave3, Gather.wave4, Gather.wave5):
-        for group in groups:
-            wave(group)
-    for other in quad_peers:
-        for k in range(4):
-            remote(
-                res_hbm.at[:, columns_of(other, k)],
-                rbuf.at[quad, :, pl.ds(k * share, share)],
-                r_send,
-                r_recv.at[quad],
-                fsdp=other,
-            )
-
-    @pl.loop(1, GROUP)
-    def _(j):
-        remote(idbuf.at[me], idbuf.at[me], id_send, id_recv.at[me], fsdp=(me + j) % GROUP)
-
-
-    @pl.loop(0, PIECES)
-    def _(p):
-        send_w(z, 1, p, device(0, 1, 0), own=True)
-        send_w(z, 0, p, device(0, 3, 0), own=True)
-
-    locals_[1].wait()
-    arrived(qbuf.at[1 - x], q_recv)
-
-    for g in range(2):
+
+    def choose(g):
+        wait_rest(*doc, 2 * g, 2 * g + 1)
+        for p in (2 * g, 2 * g + 1):
+            doc_locals[p].wait()
+        kv[me, pl.ds(2 * g, 2)] = (doc_a, doc_b)[g][source[row]]
+        groups[g].wave1()
+
+    def attend(g):
         groups[g].last(0, 4)
 
         @pl.loop(0, GROUP // 2)
         def _(k):
             for half in range(2):
-                groups[g].wait(2 * k + 1 - core, half * 2 + g)
+                groups[g].wait(2 * k + 1 - core, 2 * g + half)
 
         @pl.loop(0, HEADS // 2, unroll=4)
         def _(h):
             columns = pl.ds(pl.multiple_of(h * DEPTH, DEPTH), DEPTH)
             whole = pl.ds(pl.multiple_of(h * DEPTH + g * half_width, DEPTH), DEPTH)
-            keys = kv[:, g, :, columns].reshape(-1, DEPTH)
-            values = kv[:, 2 + g, :, columns].reshape(-1, DEPTH)
+            keys = kv[:, 2 * g, :, columns].reshape(-1, DEPTH)
+            values = kv[:, 2 * g + 1, :, columns].reshape(-1, DEPTH)
             scores = lax.dot_general(
                 qbuf[:, :, whole].reshape(-1, DEPTH),
                 keys,
@@ -350,15 +359,56 @@
         done = att.at[core, :, :, pl.ds(g * half_width, half_width)]
         remote(done, done, att_send, att_recv.at[g], fsdp=device(0, 0, 1))
 
-    for copy in locals_[2:]:
+    choose(0)
+    relay(*doc, 2, 3)
+    for p in range(4):
+        wait_row(*part, row, p)
+        send_row(*part, row, p, partner, up, down)
+    groups[0].wave2()
+    groups[0].wave3()
+    choose(1)
+    for other in quad_peers:
+        for k in range(4):
+            remote(
+                res_hbm.at[:, columns_of(other, k)],
+                rbuf.at[quad, :, pl.ds(k * share, share)],
+                r_send,
+                r_recv.at[quad],
+                fsdp=other,
+            )
+
+    groups[0].wave4()
+    groups[0].wave5()
+    groups[1].wave2()
+    groups[1].wave3()
+    for p in range(4):
+        wait_row(*part, partner, p)
+        send_row(*part, partner, p, up, down)
+    locals_[0].wait()
+    arrived(qbuf.at[1 - x], q_recv)
+    attend(0)
+    groups[1].wave4()
+    groups[1].wave5()
+    relay(*part, 0, 1)
+    relay(*part, 2, 3)
+    @pl.loop(1, GROUP)
+    def _(j):
+        remote(idbuf.at[me], idbuf.at[me], id_send, id_recv.at[me], fsdp=(me + j) % GROUP)
+
+
+    attend(1)
+
+    for copy in locals_[1:]:
         copy.wait()
 
     @pl.loop(0, PIECES)
     def _(p):
-        wait_w(zp, 0, p)
-        wait_w(zm, 1, p)
-        wait_w((z + 2) % 4, 0, p)
-        wait_w((z + 2) % 4, 1, p)
+        rows = pl.ds(p * w_rows, w_rows)
+        arrived(wbuf.at[below, 0, rows], w_recv.at[0, p])
+        arrived(wbuf.at[above, 1, rows], w_recv.at[1, p])
+
+    wait_rest(*part, 0, 1)
+    wait_rest(*part, 2, 3)
 
     for other in quad_peers:
         slot = (other // 8) * 2 + other % 2
@@ -366,55 +416,60 @@
     for g in range(2):
         arrived(att.at[1 - core, :, :, pl.ds(g * half_width, half_width)], att_recv.at[g])
 
-    def project(k, squares):
-        columns = pl.ds(pl.multiple_of(k * share, share), share)
-        weight = wbuf[k].reshape(-1, share)
-        mixed = jnp.dot(att[...].reshape(4 * tokens, -1), weight, preferred_element_type=jnp.float32)
-        out = []
-        for slot in range(4):
-            start = ((slot % 2) * 2 + slot // 2) * tokens
-            part = mixed[start : start + tokens] + rbuf[slot, :, columns].astype(jnp.float32)
-            summed[slot, :, columns] = part
-            out.append(squares[slot] + part * part)
-        return tuple(out)
-
-    zero = jnp.zeros((tokens, share), jnp.float32)
-    squares = lax.fori_loop(0, 4, project, (zero,) * 4)
-    for slot in range(4):
-        own = jnp.sum(squares[slot], axis=1, keepdims=True)
-        sq_out[slot] = jnp.broadcast_to(own, (tokens, 128)).T[0:8]
-    for other in quad_peers:
-        remote(sq_out, sq_in.at[quad], sq_send, sq_recv.at[quad], fsdp=other)
-    sq_in[quad] = sq_out[...]
-    for other in quad_peers:
-        slot = (other // 8) * 2 + other % 2
-        arrived(sq_in.at[slot], sq_recv.at[slot])
-    mean = (sq_in[0] + sq_in[1] + sq_in[2] + sq_in[3]) / head_hbm.shape[1]
-    scale = lax.rsqrt(mean + 1e-06)
-    for slot in range(4):
-        factor = jnp.broadcast_to(scale[slot, 0:1], (128, tokens)).T[:, 0:1]
-        for k in range(4):
-            columns = pl.ds(k * share, share)
-            hidden = summed[slot, :, columns] * factor * gain[:, columns_of(me, k)]
-            spot = pl.ds(pl.multiple_of((quad * 4 + k) * share, share), share)
-            rows = pl.ds((slot // 2) * 2 * tokens + (slot % 2) * tokens, tokens)
-            hbuf[z, rows, spot] = hidden.astype(jnp.bfloat16)
-
-    piece = hbuf.shape[1] // HIDDEN
-    quarter = hbuf.shape[2] // 4
+    piece = 2 * hbuf.shape[2] // HIDDEN
+    quarter = hbuf.shape[3] // 4
 
     def hidden_view(slot, p):
         place = (slot // 8) * 2 + slot % 2
         return hbuf.at[
             (slot // 2) % 4,
-            pl.ds(p * piece, piece),
+            p // (HIDDEN // 2),
+            pl.ds(p % (HIDDEN // 2) * piece, piece),
             pl.ds(pl.multiple_of(place * quarter, quarter), quarter),
         ]
 
     hg = Gather(
         me, hidden_view, lambda p: hidden_view(me, p), h_send, h_recv, (0, VIA_X), (VIA_X, HIDDEN)
     )
-    hg.wave1()
+    def project(chip):
+        def step(k, squares):
+            columns = pl.ds(pl.multiple_of(k * share, share), share)
+            weight = wbuf[k].reshape(-1, share)
+            mixed = jnp.dot(
+                att[:, chip].reshape(2 * tokens, -1), weight, preferred_element_type=jnp.float32
+            )
+            base = jnp.concatenate([rbuf[2 * chip + c, :, columns] for c in range(2)])
+            total = mixed + base.astype(jnp.float32)
+            summed[chip, :, columns] = total
+            return squares + total * total
+
+        squares = lax.fori_loop(0, 4, step, jnp.zeros((2 * tokens, share), jnp.float32))
+        own = jnp.sum(squares, axis=1, keepdims=True)
+        sq_out[chip] = jnp.broadcast_to(own, (2 * tokens, 128)).T[0:8]
+        for other in quad_peers:
+            remote(
+                sq_out.at[chip], sq_in.at[chip, quad], sq_send, sq_recv.at[chip, quad], fsdp=other
+            )
+        sq_in[chip, quad] = sq_out[chip]
+
+    def normalize(chip):
+        for other in quad_peers:
+            slot = (other // 8) * 2 + other % 2
+            arrived(sq_in.at[chip, slot], sq_recv.at[chip, slot])
+        mean = jnp.sum(sq_in[chip, :, 0:1], axis=0) / head_hbm.shape[1]
+        scale = lax.rsqrt(mean + 1e-06)
+        factor = jnp.broadcast_to(scale, (128, 2 * tokens)).T[:, 0:1]
+        for k in range(4):
+            columns = pl.ds(k * share, share)
+            hidden = summed[chip, :, columns] * factor * gain[:, columns_of(me, k)]
+            spot = pl.ds(pl.multiple_of((quad * 4 + k) * share, share), share)
+            hbuf[z, chip, :, spot] = hidden.astype(jnp.bfloat16)
+        hg.wave1(chip * HIDDEN // 2, (chip + 1) * HIDDEN // 2)
+
+    project(0)
+    project(1)
+    normalize(0)
+    normalize(1)
     arrived(head, head_sem)
 
     @pl.loop(1, GROUP)
@@ -426,14 +481,12 @@
 
     parts = HIDDEN // 4
 
-    def finish(spot, start, count):
-        rows = pl.ds(start, count * tokens)
-        logits[:, : count * tokens] = lax.dot_general(
-            head[...], hbuf[spot, rows], (((1,), (1,)), ((), ())), preferred_element_type=jnp.float32
+    def finish(rows, slots):
+        logits[...] = lax.dot_general(
+            head[...], rows, (((1,), (1,)), ((), ())), preferred_element_type=jnp.float32
         )
-        for c in range(count):
-            index = start // tokens + c
-            slot = (index // 2) * 8 + spot * 2 + index % 2
+        for c in range(2):
+            slot = slots[c]
             block = logits[:, c * tokens : (c + 1) * tokens]
             largest = jnp.max(block, axis=0, keepdims=True)
             total = jnp.sum(jnp.exp(block - largest), axis=0, keepdims=True)
@@ -456,21 +509,28 @@
     def _(step):
         for when, wave in ((0, hg.wave2), (1, hg.wave3), (2, hg.wave4), (4, hg.wave5)):
             pl.when(step == when)(wave)
-        half = jnp.where(step < 2, step, (step - 2) // 2)
+        chip = jnp.where(step < 2, step, (step - 2) // 2)
         dz = jnp.where(step < 2, 0, 1 + 2 * (step % 2))
         spot = (z + dz) % 4
-        wait_other_core(spot, half * 2 * parts, half * 2 * parts + 2 * parts)
-        finish(spot, half * 2 * tokens, 2)
-
-    def last_quarter(step):
-        quarter_of = (step % 2) * 2 + step // 2
-        for k in range(4):
-            pl.when(quarter_of == k)(lambda: hg.last(k * parts, (k + 1) * parts))
-        wait_other_core(spot, quarter_of * parts, quarter_of * parts + parts)
-        finish(spot, quarter_of * tokens, 1)
+        wait_other_core(spot, chip * 2 * parts, chip * 2 * parts + 2 * parts)
+        slot = chip * 8 + spot * 2
+        finish(hbuf[spot, chip], (slot, slot + 1))
 
     spot = (z + 2) % 4
-    pl.loop(0, 4)(last_quarter)
+
+    @pl.loop(0, 2)
+    def _(c):
+        for k in range(2):
+
+            @pl.when(c == k)
+            def _():
+                hg.last(k * parts, k * parts + parts)
+                hg.last((2 + k) * parts, (3 + k) * parts)
+
+        wait_other_core(spot, c * parts, c * parts + parts)
+        wait_other_core(spot, (2 + c) * parts, (2 + c) * parts + parts)
+        rows = hbuf[spot, :, pl.ds(pl.multiple_of(c * tokens, tokens), tokens)]
+        finish(rows.reshape(2 * tokens, -1), (spot * 2 + c, 8 + spot * 2 + c))
 
     stat_in[me] = stat_out[me]
 
@@ -491,15 +551,16 @@
     gap = jnp.clip(before - new, -3.0, 3.0)
     kl_out[...] = jnp.where(live, jnp.exp(gap) - gap - 1.0, 0.0)
 
-    arrived(hbuf.at[:, pl.ds(0, 15 * hbuf.shape[1] // 16)], h_send)
+    arrived(sq_in.at[:, pl.ds(0, 3)], sq_send)
+    arrived(hbuf.at[:, :, pl.ds(0, 15 * hbuf.shape[2] // 16)], h_send)
     for buf, count, sem in (
         (kv, 15, kv_send),
-        (wbuf, 3, w_send),
-        (dbuf, 7, dp_send),
+        (wbuf, 1, w_send),
+        (wbuf, 2, ws_send),
+        (kv, 7, dp_send),
         (rbuf, 3, r_send),
         (qbuf, 1, q_send),
         (att, 1, att_send),
-        (sq_in, 3, sq_send),
         (idbuf, 15, id_send),
         (stat_out, 15, stat_send),
     ):
@@ -528,29 +589,32 @@
         scratch_shapes=[
             pltpu.VMEM(head.shape, bf16),
             pltpu.VMEM((4, 2, width // 2, share), bf16),
-            pltpu.VMEM((4, 4 * tokens, columns), bf16),
-            pltpu.VMEM((ROWS, 2, positions, width), bf16),
+            pltpu.VMEM((4, 2, 2 * tokens, columns), bf16),
+            pltpu.VMEM((ROWS, 2, positions, width // 2), bf16),
+            pltpu.VMEM((ROWS, 2, positions, width // 2), bf16),
             pltpu.VMEM((GROUP, 4, positions, width // 2), bf16),
             pltpu.VMEM((2, tokens, width), bf16),
             pltpu.VMEM((4, tokens, columns // 4), bf16),
             pltpu.VMEM((2, 2, tokens, width), bf16),
-            pltpu.VMEM((4, tokens, columns // 4), f32),
+            pltpu.VMEM((2, 2 * tokens, columns // 4), f32),
             pltpu.VMEM((head.shape[0], 256), f32),
             pltpu.VMEM((GROUP, 8, 128), jnp.int32),
-            pltpu.VMEM((4, 8, 128), f32),
-            pltpu.VMEM((4, 4, 8, 128), f32),
+            pltpu.VMEM((2, 8, 2 * tokens), f32),
+            pltpu.VMEM((2, 4, 8, 2 * tokens), f32),
             pltpu.VMEM((GROUP, 8, 128), f32),
             pltpu.VMEM((GROUP, 8, 128), f32),
-            dma((7,)),
-            dma,
-            dma,
-            dma((4, 2, PIECES)),
+            dma((10,)),
+            dma,
+            dma,
+            dma((2, PIECES)),
+            dma,
+            dma((ROWS, 4)),
             dma,
             dma((GROUP, HIDDEN)),
             dma,
             dma((GROUP, 4)),
             dma,
-            dma((ROWS, 2)),
+            dma((ROWS, 4)),
             dma,
             dma,
             dma,
@@ -558,7 +622,7 @@
             dma,
             dma((2,)),
             dma,
-            dma((4,)),
+            dma((2, 4)),
             dma,
             dma((GROUP,)),
             dma,

time: 144 us -> 132 us (0.917); the launches traced: 142 us -> 132 us
  Pallas kernels: 140 us -> 129 us
    pallas_call x1, Pallas kernels: 140 us -> 129 us  [on_device(): pl.pallas_call(kernel, out_shape=(out, out), in_specs=[smem, smem, vmem,...]
where the time goes in v4:
time: 132 us
  Pallas kernels  129 us (98%)
  local copies, waits for them, and re-layouts  2.25 us (2%)
    pallas_call x1, Pallas kernels, on_device(): pl.pallas_call(kernel, out_shape=(out, out), in_specs=[smem, smem, vmem,...  129 us

profile of v4, /device:TPU:1, one launch (start us, length us, event | category | flops | bytes accessed | tf_op | source)
XLA Modules:
  0.0 132.0 jit_solution(9731869306349122043)
XLA Ops:
  0.6 129.1 %shard_map.113 = (f32[1,128]{1,0:T(1,128)}, f32[1,128]{1,0:T(1,128)}) custom-call(s32[8]{0:T(128)} %source.1, s32[1,8]{1,0:T(1,128)} %lengths.1, s32[1,128]{1,0:T(1,128)} %bitcast.10, f32[1,128]{1,0:T(1,128)} %bitcast.11, f32[1,4096]{1,0:T(1,128)} %bitcast.9, bf16[128,2048]{1,0:T(8,128)(2,1)} %q_hbm.1, bf16[2,32,2048]{2,1,0:T(8,128)(2,1)} %bitcast.8, ...), custom_call_target="tpu_custom_call" | custom-call | tf_op jit(solution)/shard_map/pallas_call | solution.py:584
  129.7 1.1 copy.14
  130.8 1.1 copy.15

commit v5 on v4

--- a/solution.py
+++ b/solution.py
@@ -123,8 +123,7 @@
     res_hbm,
     w_hbm,
     head_hbm,
-    ratio_out,
-    kl_out,
+    out,
     head,
     wbuf,
     hbuf,
@@ -547,9 +546,9 @@
     position = core * tokens + lax.broadcasted_iota(jnp.int32, (1, 128), 1)
     live = position < lengths[0, me // 2]
     before = old[...]
-    ratio_out[...] = jnp.where(live, new - before, 0.0)
+    out[0:1] = jnp.where(live, new - before, 0.0)
     gap = jnp.clip(before - new, -3.0, 3.0)
-    kl_out[...] = jnp.where(live, jnp.exp(gap) - gap - 1.0, 0.0)
+    out[1:2] = jnp.where(live, jnp.exp(gap) - gap - 1.0, 0.0)
 
     arrived(sq_in.at[:, pl.ds(0, 3)], sq_send)
     arrived(hbuf.at[:, :, pl.ds(0, 15 * hbuf.shape[2] // 16)], h_send)
@@ -580,12 +579,11 @@
     vmem = pl.BlockSpec(memory_space=pltpu.VMEM)
     any_ = pl.BlockSpec(memory_space=pl.ANY)
     dma = pltpu.SemaphoreType.DMA
-    out = jax.ShapeDtypeStruct((1, tokens), f32)
-    ratio, kl = pl.pallas_call(
+    both = pl.pallas_call(
         kernel,
-        out_shape=(out, out),
+        out_shape=jax.ShapeDtypeStruct((2, tokens), f32),
         in_specs=[smem, smem, vmem, vmem, vmem] + [any_] * 5,
-        out_specs=(vmem, vmem),
+        out_specs=vmem,
         scratch_shapes=[
             pltpu.VMEM(head.shape, bf16),
             pltpu.VMEM((4, 2, width // 2, share), bf16),
@@ -643,7 +641,7 @@
         out_weight.reshape(2, width // 2, share),
         head,
     )
-    return ratio.reshape(tokens), kl.reshape(tokens)
+    return both[0], both[1]
 
 
 def solution(mesh):

time: 132 us -> 131 us (level)
    unnamed x2 -> x0, local copies, waits for them, and re-layouts: 2.25 us -> none
where the time goes in v5:
time: 131 us
  Pallas kernels  129 us (98%)
    pallas_call x1, Pallas kernels, on_device(): pl.pallas_call(kernel, out_shape=jax.ShapeDtypeStruct((2, tokens), f32),...  129 us

profile of v5, /device:TPU:1, one launch (start us, length us, event | category | flops | bytes accessed | tf_op | source)
XLA Modules:
  0.0 131.0 jit_solution(10244202504356985343)
XLA Ops:
  0.6 129.1 %shard_map.113 = f32[2,128]{1,0:T(2,128)} custom-call(s32[8]{0:T(128)} %source.1, s32[1,8]{1,0:T(1,128)} %lengths.1, s32[1,128]{1,0:T(1,128)} %bitcast.12, f32[1,128]{1,0:T(1,128)} %bitcast.13, f32[1,4096]{1,0:T(1,128)} %bitcast.11, bf16[128,2048]{1,0:T(8,128)(2,1)} %q_hbm.1, bf16[2,32,2048]{2,1,0:T(8,128)(2,1)} %bitcast.10, bf16[128,4096]{1,0:T(8,128)(2,1)} %res_hbm.1, ...), custom_call_target="tpu_custom_call" | custom-call | tf_op jit(solution)/shard_map/pallas_call | solution.py:582
  129.8 1.3 slice_bitcast_fusion

commit v6 on v5

--- a/solution.py
+++ b/solution.py
@@ -81,8 +81,8 @@
             self.pass_on(self.zm, p, self.zp)
             self.pass_on(self.zp, p)
 
+        self.each(self.second[0], self.middle, down)
         self.each(self.middle, self.second[1], up)
-        self.each(self.second[0], self.middle, down)
         self.each(*self.first, own_side)
         self.each(*self.second, lambda p: self.pass_on(self.x, p))
 
@@ -225,12 +225,6 @@
     ]
     for copy in doc_locals + locals_:
         copy.start()
-    for k in range(GROUP):
-        pltpu.make_async_copy(
-            head_hbm.at[:, pl.ds(k * share, share)],
-            head.at[:, pl.ds(((k // 8 * 2 + k % 2) * 4 + k // 2 % 4) * share, share)],
-            head_sem,
-        ).start()
     idbuf[me] = jnp.broadcast_to(ids[...], (8, 128))
 
     pl.semaphore_wait(barrier, GROUP - 1 + 3)
@@ -297,6 +291,13 @@
     def _(p):
         send_w(0, p, device(0, 1, 0))
         send_w(1, p, device(0, 3, 0))
+
+    for k in range(GROUP):
+        pltpu.make_async_copy(
+            head_hbm.at[:, pl.ds(k * share, share)],
+            head.at[:, pl.ds(((k // 8 * 2 + k % 2) * 4 + k // 2 % 4) * share, share)],
+            head_sem,
+        ).start()
 
     for p in (0, 1):
         wait_row(*doc, partner, p)
@@ -390,11 +391,6 @@
     groups[1].wave5()
     relay(*part, 0, 1)
     relay(*part, 2, 3)
-    @pl.loop(1, GROUP)
-    def _(j):
-        remote(idbuf.at[me], idbuf.at[me], id_send, id_recv.at[me], fsdp=(me + j) % GROUP)
-
-
     attend(1)
 
     for copy in locals_[1:]:
@@ -442,7 +438,7 @@
             summed[chip, :, columns] = total
             return squares + total * total
 
-        squares = lax.fori_loop(0, 4, step, jnp.zeros((2 * tokens, share), jnp.float32))
+        squares = lax.fori_loop(0, 4, step, jnp.zeros((2 * tokens, share), jnp.float32), unroll=True)
         own = jnp.sum(squares, axis=1, keepdims=True)
         sq_out[chip] = jnp.broadcast_to(own, (2 * tokens, 128)).T[0:8]
         for other in quad_peers:
@@ -467,6 +463,11 @@
 
     project(0)
     project(1)
+
+    @pl.loop(1, GROUP)
+    def _(j):
+        remote(idbuf.at[me], idbuf.at[me], id_send, id_recv.at[me], fsdp=(me + j) % GROUP)
+
     normalize(0)
     normalize(1)
     arrived(head, head_sem)

time: 131 us -> 131 us (level)
  no operation moved by 1% of the time
where the time goes in v6:
time: 131 us; the launch traced here: 130 us
  Pallas kernels  129 us (98%)
    pallas_call x1, Pallas kernels, on_device(): pl.pallas_call(kernel, out_shape=jax.ShapeDtypeStruct((2, tokens), f32),...  129 us

profile of v6, /device:TPU:1, one launch (start us, length us, event | category | flops | bytes accessed | tf_op | source)
XLA Modules:
  0.0 130.4 jit_solution(16269114581022534782)
XLA Ops:
  0.6 128.5 %shard_map.113 = f32[2,128]{1,0:T(2,128)} custom-call(s32[8]{0:T(128)} %source.1, s32[1,8]{1,0:T(1,128)} %lengths.1, s32[1,128]{1,0:T(1,128)} %bitcast.12, f32[1,128]{1,0:T(1,128)} %bitcast.13, f32[1,4096]{1,0:T(1,128)} %bitcast.11, bf16[128,2048]{1,0:T(8,128)(2,1)} %q_hbm.1, bf16[2,32,2048]{2,1,0:T(8,128)(2,1)} %bitcast.10, bf16[128,4096]{1,0:T(8,128)(2,1)} %res_hbm.1, ...), custom_call_target="tpu_custom_call" | custom-call | tf_op jit(solution)/shard_map/pallas_call | solution.py:583
  129.2 1.3 slice_bitcast_fusion
